TPU v7x, 128 devices: a whole 4x4x4 slice. The times are simulated.
128 devices in a mesh: ta: 4 (over y_hi, core), gy: 32 (over y_lo, z, x).
Axes of the slice: x: 4, y: 4 (y_hi: 2, y_lo: 2; y = y_hi * 2 + y_lo), z: 4, core: 2. Of those that a mesh axis runs over, the one named last changes fastest.
Arguments:
- charge_field: bfloat16 [32, 2048, 2048], P('ta', 'gy'), may hold values from -324 to 324
Outputs:
- spectrum: float32 [32, 2048, 2048], P(None, 'gy', 'ta')
All inputs are finite; a program needn't handle non-finite values.
Results may differ from a plain program's by a relative error of at most 0.023.
Values may be sent and summed in bfloat16 or wider, within the bound.
A program may use at most 128 MiB of HBM per device.

v0:
```python
import math

import jax
import jax.numpy as jnp
from jax import lax
from jax.sharding import PartitionSpec as P

NX = 2048
NY = 2048
PX = 32
PY = 32


def dft_tables(length, rows_idx, cols_idx):
    phases = rows_idx[:, None] * cols_idx[None, :] % length
    angles = phases.astype(jnp.float32) * (2.0 * math.pi / length)
    return (jnp.cos(angles).astype(jnp.bfloat16), jnp.sin(angles).astype(jnp.bfloat16))


def time_tables(count):
    places = jnp.arange(count, dtype=jnp.int32)
    phases = places[:, None] * places[None, :] % count
    angles = phases.astype(jnp.float32) * (2.0 * math.pi / count)
    window = 0.5 - 0.5 * jnp.cos((places.astype(jnp.float32) + 0.5) * (2.0 * math.pi / count))
    cos_w = (jnp.cos(angles) * window[None, :]).astype(jnp.bfloat16)
    sin_w = (jnp.sin(angles) * window[None, :]).astype(jnp.bfloat16)
    return (cos_w, sin_w, jnp.sum(window * window))


def factored(real_in, imag_in, first):
    rows, length = real_in.shape
    second = length // first
    idx_a = jnp.arange(first, dtype=jnp.int32)
    idx_b = jnp.arange(second, dtype=jnp.int32)
    cos_a, sin_a = dft_tables(first, idx_a, idx_a)
    cos_b, sin_b = dft_tables(second, idx_b, idx_b)
    cos_t, sin_t = dft_tables(length, idx_a, idx_b)
    cos_t = cos_t.astype(jnp.float32)
    sin_t = sin_t.astype(jnp.float32)
    real_r = real_in.reshape(rows, first, second)
    first_real = jnp.einsum("rab,ak->rkb", real_r, cos_a, preferred_element_type=jnp.float32)
    first_imag = -jnp.einsum("rab,ak->rkb", real_r, sin_a, preferred_element_type=jnp.float32)
    if imag_in is not None:
        imag_r = imag_in.reshape(rows, first, second)
        first_real = first_real + jnp.einsum(
            "rab,ak->rkb", imag_r, sin_a, preferred_element_type=jnp.float32
        )
        first_imag = first_imag + jnp.einsum(
            "rab,ak->rkb", imag_r, cos_a, preferred_element_type=jnp.float32
        )
    first_real = first_real.astype(jnp.bfloat16).astype(jnp.float32)
    first_imag = first_imag.astype(jnp.bfloat16).astype(jnp.float32)
    turn_real = (first_real * cos_t + first_imag * sin_t).astype(jnp.bfloat16)
    turn_imag = (first_imag * cos_t - first_real * sin_t).astype(jnp.bfloat16)
    out_real = jnp.einsum(
        "rkn,nm->rmk", turn_real, cos_b, preferred_element_type=jnp.float32
    ) + jnp.einsum("rkn,nm->rmk", turn_imag, sin_b, preferred_element_type=jnp.float32)
    out_imag = jnp.einsum(
        "rkn,nm->rmk", turn_imag, cos_b, preferred_element_type=jnp.float32
    ) - jnp.einsum("rkn,nm->rmk", turn_real, sin_b, preferred_element_type=jnp.float32)
    return (
        out_real.reshape(rows, length).astype(jnp.bfloat16),
        out_imag.reshape(rows, length).astype(jnp.bfloat16),
    )


def x_transform(charge_field):
    frames_here, rows_here, length = charge_field.shape
    flat_rows = charge_field.reshape(frames_here * rows_here, length)
    real_x, imag_x = factored(flat_rows, None, PX)
    return jnp.stack([real_x, imag_x]).reshape(2, frames_here, rows_here, length)


def y_rows(regrouped):
    frames_all, kx_here, length = (regrouped.shape[1], regrouped.shape[2], regrouped.shape[3])
    real_in = regrouped[0].reshape(frames_all * kx_here, length)
    imag_in = regrouped[1].reshape(frames_all * kx_here, length)
    real_y, imag_y = factored(real_in, imag_in, PY)
    return jnp.stack([real_y, imag_y]).reshape(2, frames_all, kx_here, length)


def power(relaid):
    cos_t, sin_t, wsum = time_tables(relaid.shape[1])
    real_in = relaid[0]
    imag_in = relaid[1]
    real_t = jnp.einsum(
        "wt,txk->wxk", cos_t, real_in, preferred_element_type=jnp.float32
    ) + jnp.einsum("wt,txk->wxk", sin_t, imag_in, preferred_element_type=jnp.float32)
    imag_t = jnp.einsum(
        "wt,txk->wxk", cos_t, imag_in, preferred_element_type=jnp.float32
    ) - jnp.einsum("wt,txk->wxk", sin_t, real_in, preferred_element_type=jnp.float32)
    return (real_t * real_t + imag_t * imag_t) / (NX * NY * wsum)


def shards(charge_field):
    spectra_x = x_transform(charge_field)
    turned = jnp.transpose(spectra_x, (0, 1, 3, 2))
    regrouped = lax.all_to_all(turned, "gy", split_axis=2, concat_axis=3, tiled=True)
    spectra_y = y_rows(regrouped)
    relaid = lax.all_to_all(spectra_y, "ta", split_axis=3, concat_axis=1, tiled=True)
    return power(relaid)


def solution(mesh):
    placed = (P("ta", "gy", None),)
    return jax.shard_map(
        shards, mesh=mesh, in_specs=placed, out_specs=P(None, "gy", "ta"), check_vma=False
    )
```

profile of v0, /device:TPU:1, one launch (start us, length us, event | category | flops | bytes accessed | tf_op | source)
XLA Modules:
  0.0 333.6 jit_solution(3063569727668128835)
XLA Ops:
  0.1 7.1 %reshape_reshape.3 = bf16[512,32,64]{2,1,0:T(8,128)(2,1)} reshape(bf16[8,64,2048]{2,1,0:T(8,128)(2,1)} %param.1) | data formatting | bytes 4194304 | tf_op jit(solution)/shard_map/reshape;reshape | solution.py:40
  7.2 5.8 %copy.47 = bf16[512,32,64]{0,1,2:T(8,128)(2,1)S(1)} copy(bf16[512,32,64]{2,1,0:T(8,128)(2,1)} %reshape_reshape.3) | data formatting | bytes 4194304 | tf_op jit(solution)/shard_map/reshape;reshape | solution.py:40
  18.7 4.9 %fusion.29 = f32[64,512,32]{1,0,2:T(8,128)} fusion(bf16[512,32,64]{0,1,2:T(8,128)(2,1)S(1)} %get-tuple-element.10), kind=kOutput, calls=%fused_computation.48 | convolution fusion | flops 134279168 | bytes 6291456 | tf_op jit(solution)/shard_map/rkn,nm->rmk/dot_general | solution.py:58
  23.5 2.9 fusion.35
  29.0 6.4 %convert_element_type.318 = bf16[1,8,64,2048]{2,1,3,0:T(8,128)(2,1)} reshape(bf16[512,64,32]{0,2,1:T(8,128)(2,1)} %copy.52) | data formatting | bytes 4194304 | tf_op jit(solution)/shard_map/convert_element_type | solution.py:62
  35.4 5.1 %fusion.38 = bf16[512,64,32]{0,1,2:T(8,128)(2,1)S(1)} fusion(f32[64,512,32]{1,0,2:T(8,128)} %fusion.29, bf16[512,32,64]{0,1,2:T(8,128)(2,1)S(1)} %copy-done.1), kind=kOutput, calls=%fused_computation.55 | convolution fusion | flops 136376320 | bytes 8388608 | tf_op jit(solution)/shard_map/rkn,nm->rmk/dot_general | solution.py:60
  41.7 3.6 %convert_element_type.321 = bf16[1,8,64,2048]{2,1,3,0:T(8,128)(2,1)} reshape(bf16[512,64,32]{0,2,1:T(8,128)(2,1)S(1)} %copy.55) | data formatting | bytes 4194304 | tf_op jit(solution)/shard_map/convert_element_type | solution.py:63
  45.3 7.6 %copy_bitcast_fusion.1 = bf16[2048,2,8,64]{3,2,1,0:T(8,128)(2,1)} fusion(bf16[1,8,64,2048]{2,1,3,0:T(8,128)(2,1)} %convert_element_type.321, bf16[1,8,64,2048]{2,1,3,0:T(8,128)(2,1)} %convert_element_type.318), kind=kLoop, calls=%fused_computation.186 | loop fusion | flops 2097152 | bytes 8388608
  52.9 13.9 %reshape.125 = bf16[32,2,32768]{2,1,0:T(2,128)(2,1)} reshape(bf16[2048,2,8,64]{3,2,1,0:T(8,128)(2,1)} %copy_bitcast_fusion.1) | data formatting | bytes 8388608
  66.8 59.7 %all_to_all.30 = bf16[32,2,32768]{2,1,0:T(2,128)(2,1)} all-to-all(bf16[32,2,32768]{2,1,0:T(2,128)(2,1)} %reshape.125), channel_id=1, replica_groups=mesh['ta'=4,'gy'=32] {'gy'}, dimensions={0} | all-to-all | bytes 8388608 | tf_op jit(solution)/shard_map/all_to_all | solution.py:98
  126.4 13.7 %reshape.126 = bf16[2048,2,8,64]{3,2,1,0:T(8,128)(2,1)} reshape(bf16[32,2,32768]{2,1,0:T(2,128)(2,1)} %all_to_all.30) | data formatting | bytes 8388608
  140.1 11.8 %copy.84 = bf16[2,8,32,64,64]{3,2,4,1,0:T(8,128)(2,1)} copy(bf16[2,8,32,64,64]{4,1,0,3,2:T(8,128)(2,1)} %bitcast.105) | data formatting | bytes 8388608 | tf_op jit(solution)/shard_map/all_to_all | solution.py:98
  151.9 5.5 %fusion.173 = (bf16[1,8,64,32,64]{2,3,4,1,0:T(8,128)(2,1)}, bf16[1,8,64,32,64]{2,3,4,1,0:T(8,128)(2,1)S(1)}) fusion(bf16[2,8,64,32,64]{2,3,4,1,0:T(8,128)(2,1)} %bitcast.104), kind=kLoop, calls=%fused_computation.183 | loop fusion | bytes 8388608 | tf_op jit(solution)/shard_map/slice | solution.py:77
  157.5 6.8 %copy.58 = bf16[1,8,64,32,64]{2,1,3,4,0:T(8,128)(2,1)} copy(bf16[1,8,64,32,64]{2,3,4,1,0:T(8,128)(2,1)S(1)} %get-tuple-element.6) | data formatting | bytes 4194304 | tf_op jit(solution)/shard_map/slice | solution.py:76
  164.3 5.8 %reshape_reshape_squeeze.6 = bf16[512,32,64]{0,1,2:T(8,128)(2,1)S(1)} reshape(bf16[1,8,64,32,64]{2,1,3,4,0:T(8,128)(2,1)} %copy.58) | data formatting | bytes 4194304 | tf_op jit(solution)/shard_map/reshape;reshape;squeeze | solution.py:40
  176.2 6.9 %copy.60 = bf16[1,8,64,32,64]{2,1,3,4,0:T(8,128)(2,1)} copy(bf16[1,8,64,32,64]{2,3,4,1,0:T(8,128)(2,1)S(1)} %copy-done.4) | data formatting | bytes 4194304 | tf_op jit(solution)/shard_map/slice | solution.py:77
  183.0 5.6 %reshape_reshape_squeeze.7 = bf16[512,32,64]{0,1,2:T(8,128)(2,1)S(1)} reshape(bf16[1,8,64,32,64]{2,1,3,4,0:T(8,128)(2,1)} %copy.60) | data formatting | bytes 4194304 | tf_op jit(solution)/shard_map/reshape;reshape;squeeze | solution.py:44
  189.9 3.2 add_convert_fusion.1
  193.4 3.2 fusion.9
  199.4 4.9 %fusion.23 = f32[64,512,32]{1,0,2:T(8,128)} fusion(bf16[512,32,64]{0,1,2:T(8,128)(2,1)S(1)} %get-tuple-element.8), kind=kOutput, calls=%fused_computation.42 | convolution fusion | flops 134279168 | bytes 6291456 | tf_op jit(solution)/shard_map/rkn,nm->rmk/dot_general | solution.py:58
  204.3 3.0 fusion.41
  209.9 6.4 %convert_element_type.331 = bf16[1,8,64,2048]{2,1,3,0:T(8,128)(2,1)} reshape(bf16[512,64,32]{0,2,1:T(8,128)(2,1)} %copy.66) | data formatting | bytes 4194304 | tf_op jit(solution)/shard_map/convert_element_type | solution.py:62
  216.3 5.1 %fusion.44 = bf16[512,64,32]{0,1,2:T(8,128)(2,1)S(1)} fusion(f32[64,512,32]{1,0,2:T(8,128)} %fusion.23, bf16[512,32,64]{0,1,2:T(8,128)(2,1)S(1)} %get-tuple-element.7), kind=kOutput, calls=%fused_computation.57 | convolution fusion | flops 136376320 | bytes 8388608 | tf_op jit(solution)/shard_map/rkn,nm->rmk/dot_general | solution.py:60
  222.6 3.6 %convert_element_type.334 = bf16[1,8,64,2048]{2,1,3,0:T(8,128)(2,1)} reshape(bf16[512,64,32]{0,2,1:T(8,128)(2,1)S(1)} %copy.69) | data formatting | bytes 4194304 | tf_op jit(solution)/shard_map/convert_element_type | solution.py:63
  226.2 7.6 %copy_bitcast_fusion = bf16[2048,2,8,64]{3,2,1,0:T(8,128)(2,1)} fusion(bf16[1,8,64,2048]{2,1,3,0:T(8,128)(2,1)} %convert_element_type.334, bf16[1,8,64,2048]{2,1,3,0:T(8,128)(2,1)} %convert_element_type.331), kind=kLoop, calls=%fused_computation.185 | loop fusion | flops 2097152 | bytes 8388608
  233.8 9.5 %reshape.127 = bf16[4,2,262144]{2,1,0:T(2,128)(2,1)} reshape(bf16[2048,2,8,64]{3,2,1,0:T(8,128)(2,1)} %copy_bitcast_fusion) | data formatting | bytes 8388608
  243.3 7.2 %all-to-all-start.1 = ((bf16[4,2,262144]{2,1,0:T(2,128)(2,1)}), bf16[4,2,262144]{2,1,0:T(2,128)(2,1)}, u32[]{:S(2)}, u32[]{:S(2)}) async-start(bf16[4,2,262144]{2,1,0:T(2,128)(2,1)} %reshape.127), calls=%async_computation.1 | async-start | bytes 8388608 | tf_op jit(solution)/shard_map/all_to_all | solution.py:100
  251.9 47.5 %all-to-all-done.1 = bf16[4,2,262144]{2,1,0:T(2,128)(2,1)} async-done(((bf16[4,2,262144]{2,1,0:T(2,128)(2,1)}), bf16[4,2,262144]{2,1,0:T(2,128)(2,1)}, u32[]{:S(2)}, u32[]{:S(2)}) %all-to-all-start.1) | async-done | bytes 4194336 | tf_op jit(solution)/shard_map/all_to_all | solution.py:100
  299.4 9.3 %reshape.128 = bf16[2048,2,8,64]{3,2,1,0:T(8,128)(2,1)} reshape(bf16[4,2,262144]{2,1,0:T(2,128)(2,1)} %all-to-all-done.1) | data formatting | bytes 8388608
  308.7 10.3 %copy.88 = bf16[2,8,64,4,512]{4,3,2,1,0:T(4,128)(2,1)} copy(bf16[2,8,64,4,512]{2,1,0,4,3:T(8,128)(2,1)} %bitcast.103) | data formatting | bytes 8388608 | tf_op jit(solution)/shard_map/all_to_all | solution.py:100
  319.0 3.0 fusion.174
  328.9 4.4 %copy.74 = f32[32,64,512]{2,1,0:T(8,128)} copy(f32[32,64,512]{2,0,1:T(8,128)S(1)} %add_divide_fusion) | data formatting | bytes 8388608 | tf_op jit(solution)/shard_map/div | solution.py:92
  (27 shorter events, 31.1 us)
Async XLA Ops:
  15.8 7.8 %copy-start = (bf16[512,32,64]{0,1,2:T(8,128)(2,1)}, bf16[512,32,64]{0,1,2:T(8,128)(2,1)S(1)}, u32[]{:S(2)}) copy-start(bf16[512,32,64]{0,1,2:T(8,128)(2,1)S(1)} %get-tuple-element.9) | copy-start | bytes 6291460
  26.5 8.9 %copy-start.1 = (bf16[512,32,64]{0,1,2:T(8,128)(2,1)S(1)}, bf16[512,32,64]{0,1,2:T(8,128)(2,1)}, u32[]{:S(2)}) copy-start(bf16[512,32,64]{0,1,2:T(8,128)(2,1)} %copy-done) | copy-start | bytes 6291460
  172.9 3.3 copy-start.4
  188.6 1.3 copy-start.2
  189.9 3.4 %copy-start.3 = (f32[32,512,64]{1,0,2:T(8,128)S(1)}, f32[32,512,64]{1,0,2:T(8,128)}, u32[]{:S(2)}) copy-start(f32[32,512,64]{1,0,2:T(8,128)} %fusion.85) | copy-start | bytes 12582916
  243.3 56.1 %all-to-all-start.1 = ((bf16[4,2,262144]{2,1,0:T(2,128)(2,1)}), bf16[4,2,262144]{2,1,0:T(2,128)(2,1)}, u32[]{:S(2)}, u32[]{:S(2)}) async-start(bf16[4,2,262144]{2,1,0:T(2,128)(2,1)} %reshape.127), calls=%async_computation.1 | async-start | bytes 8388608 | tf_op jit(solution)/shard_map/all_to_all | solution.py:100
where the time goes:
time: 339 us; the launch traced here: 334 us
  local copies, waits for them, and re-layouts  149 us (44%)
  blocking collectives  59.7 us (18%)
  matrix products  53.1 us (16%)
  waiting for transfers between devices  47.5 us (14%)
  other arithmetic  16.2 us (5%)
  starting transfers between devices  7.2 us (2%)
    all_to_all x1, blocking collectives, shards(): lax.all_to_all(turned, 'gy', split_axis=2, concat_axis=3, tiled=True)  59.7 us
    unnamed x14, local copies, waits for them, and re-layouts  48.4 us
    all_to_all x1, waiting for transfers between devices, shards(): lax.all_to_all(spectra_y, 'ta', split_axis=3, concat_axis=1, tiled=True)  47.5 us
    another operation x3, local copies, waits for them, and re-layouts, factored(): real_r = real_in.reshape(rows, first, second)  18.7 us
    convert_element_type x4, local copies, waits for them, and re-layouts, factored(): out_real.reshape(rows, length).astype(jnp.bfloat16)  17.8 us
    unnamed x2, other arithmetic  15.3 us
    slice x2, local copies, waits for them, and re-layouts, y_rows(): imag_in = regrouped[1].reshape(frames_all * kx_here, length)  12.4 us
    all_to_all x1, local copies, waits for them, and re-layouts, shards(): lax.all_to_all(turned, 'gy', split_axis=2, concat_axis=3, tiled=True)  11.8 us
  transfers between devices with their start and end apart: 1, of which 1 were waited for; matrix products, arithmetic and copies ran while one was open for 0% of the time, Pallas kernels for 0%

commit v1 on v0

v1 whole, which is shorter than its diff:
```python
import functools
import math

import jax
import jax.numpy as jnp
import ml_dtypes
import numpy as np
from jax import lax
from jax.experimental import pallas as pl
from jax.experimental.pallas import tpu as pltpu
from jax.sharding import PartitionSpec as P

FR, NX, NY = 32, 2048, 2048
TA, GY = 4, 32
DEV = TA * GY
FT = FR // TA
YL = NY // GY
SLOT = 8
HALF = GY // 2
F32, BF16 = jnp.float32, jnp.bfloat16
MIB = 1 << 20


def bf(a):
    return np.asarray(a).astype(np.float32).astype(ml_dtypes.bfloat16)


def device_of(group, part):
    a, h = part % TA, part // TA
    return a * GY + (group if h == 0 else GY - 1 - group)


@functools.lru_cache(None)
def x_tables():
    kx = np.zeros((2, DEV, 4), np.int64)
    for group in range(HALF):
        for part in range(8):
            for parity in range(2):
                base = 64 * group + 8 * part + parity
                kx[parity, device_of(group, part)] = base + 2 * np.arange(4)
    n = np.arange(NX // 2)
    angle = 2 * np.pi * ((kx[..., None] * n) % NX) / NX
    re, im = np.cos(angle), -np.sin(angle)
    zero = device_of(0, 0)
    im[0, zero, 0] = np.cos(np.pi * n)
    both = np.stack([re, im], axis=2)
    return bf(both.reshape(2, DEV * 8, NX // 2))


@functools.lru_cache(None)
def t_table():
    t = np.arange(FR)
    window = 0.5 - 0.5 * np.cos(2 * np.pi * (t + 0.5) / FR)
    angle = 2 * np.pi * ((t[:, None] * t[None, :]) % FR) / FR
    cw, sw = np.cos(angle) * window, np.sin(angle) * window
    out = np.zeros((2, 4, FR, FR, 2, 4))
    for p in range(4):
        out[0, p, :, :, 0, p] = cw
        out[0, p, :, :, 1, p] = sw
        out[1, p, :, :, 0, p] = -sw
        out[1, p, :, :, 1, p] = cw
    extra = np.zeros((2, FR, FR, 2, 4))
    extra[0, :, :, 1, 0] = cw
    extra[1, :, :, 1, 0] = -sw
    k = FR * 8
    return bf(np.concatenate([out.reshape(k, k), extra.reshape(2 * FR, k)])), float(np.sum(window * window))


@functools.lru_cache(None)
def y_tables():
    n, k = np.arange(NY // 4), np.arange(NY // 4)
    out = []
    for q in (0, 2, 1):
        angle = 2 * np.pi * ((n[:, None] * (4 * k[None, :] + q)) % NY) / NY
        cs = np.stack([np.cos(angle).reshape(-1, 4, 128), np.sin(angle).reshape(-1, 4, 128)], axis=2)
        out.append(cs.transpose(1, 0, 2, 3).reshape(4, NY // 4, 256))
    return bf(np.stack(out))


@functools.lru_cache(None)
def row_tables():
    direct = np.zeros((FR, 8, 2, 4, FR))
    mirror = np.zeros((FR, 8, 2, 4, FR))
    corner = np.zeros((FR, 2, 4, FR))
    for w in range(FR):
        for j in range(8):
            direct[w, j, j % 2, j // 2, w] = 1
            mirror[w, (8 - j) % 8, j % 2, j // 2, -w % FR] = 1
        corner[w, 0, 0, -w % FR] = 1
    k = FR * 8
    return bf(direct.reshape(k, k)), bf(np.concatenate([mirror.reshape(k, k), corner.reshape(FR, k)]))


@functools.lru_cache(None)
def ky_table():
    out = np.zeros((4, 128, 128, 4))
    k = np.arange(128)
    for q in range(3):
        out[q, k, k, q] = 1
    out[3, k, 127 - k, 3] = 1
    return bf(out.reshape(512, 512))


def halves(first, second):
    low = lax.broadcasted_iota(jnp.int32, first.shape, first.ndim - 1) < 64
    one = jnp.where(low, first, pltpu.roll(second, 64, first.ndim - 1))
    two = jnp.where(low, pltpu.roll(first, 64, first.ndim - 1), second)
    return one, two


NT = (((1,), (1,)), ((), ()))
X_STEPS = 4
X_ROWS = DEV * 8 // X_STEPS


def x_kernel(field, table, out, even, odd):
    @pl.when(pl.program_id(0) == 0)
    def _():
        for t in range(FT):
            lo = field[t, :, : NX // 2].astype(F32)
            hi = field[t, :, NX // 2 :].astype(F32)
            even[YL * t : YL * (t + 1)] = (lo + hi).astype(BF16)
            odd[YL * t : YL * (t + 1)] = (lo - hi).astype(BF16)

    for s in range(2):
        for r in range(0, X_ROWS, 128):
            rows = slice(r, r + 128)
            e = lax.dot_general(table[0, rows], even[256 * s : 256 * (s + 1)], NT, preferred_element_type=F32)
            o = lax.dot_general(table[1, rows], odd[256 * s : 256 * (s + 1)], NT, preferred_element_type=F32)
            for q in range(2):
                lanes = slice(128 * q, 128 * (q + 1))
                one, two = halves(e[:, lanes], o[:, lanes])
                both = jnp.concatenate([one.reshape(16, 8, 128), two.reshape(16, 8, 128)], axis=1)
                at = 16 * (2 * s + q)
                out[r // 8 : r // 8 + 16, at : at + 16] = both.astype(BF16)


def x_transform(field, table):
    return pl.pallas_call(
        x_kernel,
        grid=(X_STEPS,),
        out_shape=jax.ShapeDtypeStruct((DEV, 8 * FT, 128), BF16),
        in_specs=[
            pl.BlockSpec((FT, YL, NX), lambda s: (0, 0, 0)),
            pl.BlockSpec((2, X_ROWS, NX // 2), lambda s: (0, s, 0)),
        ],
        out_specs=pl.BlockSpec((DEV // X_STEPS, 8 * FT, 128), lambda s: (s, 0, 0)),
        scratch_shapes=[pltpu.VMEM((FT * YL, NX // 2), BF16)] * 2,
        compiler_params=pltpu.CompilerParams(vmem_limit_bytes=48 * MIB),
        name="x_transform",
    )(field, table)


def yt_kernel(scale, rec, tt, ty, rows_d, rows_m, out, corner, u0, u1, u2, u3, power_d, power_m):
    special = (lax.axis_index("ta") == 0) & (lax.axis_index("gy") == 0)
    flag = jnp.where(special, 1.0, 0.0).astype(F32)

    def time_step(q, carry):
        z = []
        for n in range(4):
            pair = 4 * n + q
            left = rec[:, 2 * pair].reshape(256, 128)
            right = rec[:, 2 * pair + 1].reshape(256, 128)
            v = jnp.dot(tt[...], jnp.concatenate([left, right], axis=1), preferred_element_type=F32)
            ve, vo = halves(v[:, :128], v[:, 128:])
            re0 = ve[:32] + flag * ve[288:320]
            im0 = ve[128:160] - flag * ve[256:288]
            re = jnp.concatenate([re0, ve[32:128], vo[:128], ve[256:288]], axis=0)
            im = jnp.concatenate([im0, ve[160:256], vo[128:256], ve[288:320]], axis=0)
            z.append((re, im))
        (ar, ai), (br, bi), (cr, ci), (dr, di) = z
        sr, si, tr, ti = ar + cr, ai + ci, br + dr, bi + di
        er, ei, fr, fi = ar - cr, ai - ci, br - dr, bi - di
        lanes = pl.ds(pl.multiple_of(128 * q, 128), 128)
        for ref, re, im in (
            (u0, sr + tr, si + ti),
            (u1, er + fi, ei - fr),
            (u2, sr - tr, si - ti),
            (u3, er - fi, ei + fr),
        ):
            ref[:288, lanes] = re.astype(BF16)
            ref[288:, lanes] = im.astype(BF16)
        return carry

    lax.fori_loop(0, 4, time_step, 0)

    def products(ref, table):
        both = jnp.dot(ref[...], table, preferred_element_type=F32)
        return both[:288, :128], both[:288, 128:], both[288:, :128], both[288:, 128:]

    def plus(p1, p2, p3, p4):
        re, im = p1 + p4, p3 - p2
        return (re * re + im * im) * scale

    def minus(p1, p2, p3, p4):
        re, im = p1 - p4, p3 + p2
        return (re * re + im * im) * scale

    def y_step(a, carry):
        def put(ref, block, quarter, value):
            lanes = pl.ds(pl.multiple_of(512 * block + 128 * quarter, 128), 128)
            ref[:, lanes] = value.astype(BF16)

        def mirrored(value):
            return jnp.concatenate([jnp.where(special, value[256:], value[:32]), value[32:256]], axis=0)

        for c, ref in ((0, u0), (2, u2)):
            parts = products(ref, ty[c // 2, a])
            put(power_d, a, c, plus(*parts)[:256])
            put(power_m, a, c, mirrored(minus(*parts)))
        up = plus(*products(u1, ty[2, a]))
        put(power_d, a, 1, up[:256])
        put(power_m, 3 - a, 3, mirrored(up))
        down = minus(*products(u3, ty[2, a]))
        put(power_m, a, 1, mirrored(down))
        put(power_d, 3 - a, 3, down[:256])
        return carry

    lax.fori_loop(0, 4, y_step, 0)

    def row_step(a, carry):
        lanes = pl.ds(pl.multiple_of(512 * a, 512), 512)
        out[a] = jnp.dot(rows_d[...], power_d[:, lanes], preferred_element_type=F32).astype(BF16)
        both = jnp.dot(rows_m[...], power_m[:, lanes], preferred_element_type=F32).astype(BF16)
        out[4 + a] = both[:256]
        corner[a] = both[256:]
        return carry

    lax.fori_loop(0, 4, row_step, 0)


def yt_transform(rec, tt, ty, rows_d, rows_m, scale):
    vm = pl.BlockSpec(memory_space=pltpu.VMEM)
    return pl.pallas_call(
        functools.partial(yt_kernel, scale),
        out_shape=(
            jax.ShapeDtypeStruct((8, 256, 512), BF16),
            jax.ShapeDtypeStruct((4, 32, 512), BF16),
        ),
        in_specs=[vm] * 5,
        out_specs=(vm, vm),
        scratch_shapes=[pltpu.VMEM((576, 512), BF16)] * 4 + [pltpu.VMEM((256, 2048), BF16)] * 2,
        compiler_params=pltpu.CompilerParams(vmem_limit_bytes=56 * MIB),
        name="yt_transform",
    )(rec, tt, ty, rows_d, rows_m)


def spread_kernel(blocks, corner, out, corner_out, send, recv, local, corner_send, corner_recv):
    a, g = lax.axis_index("ta"), lax.axis_index("gy")
    h = g // HALF
    group = jnp.where(h == 0, g, GY - 1 - g)
    part = a + TA * h

    def target(member):
        ta, th = member % TA, member // TA
        return ta, jnp.where(th == 0, group, GY - 1 - group), th

    slot_here = jnp.where(h == 0, part, 7 - part)
    own = pltpu.make_async_copy(blocks.at[part], out.at[slot_here], local)
    own.start()

    def send_one(k, carry):
        member = (part + k) % 8
        ta, tg, th = target(member)
        slot = jnp.where(th == 0, part, 7 - part)
        pltpu.make_async_remote_copy(
            src_ref=blocks.at[member],
            dst_ref=out.at[slot],
            send_sem=send,
            recv_sem=recv,
            device_id=(ta, tg),
            device_id_type=pl.DeviceIdType.MESH,
        ).start()
        return carry

    lax.fori_loop(1, 8, send_one, 0)
    has_corner = part == 0
    corner_to = GY - 1 - (group + HALF - 1) % HALF

    @pl.when(has_corner)
    def _():
        for ta in range(TA):
            pltpu.make_async_remote_copy(
                src_ref=corner.at[ta],
                dst_ref=corner_out,
                send_sem=corner_send,
                recv_sem=corner_recv,
                device_id=(ta, corner_to),
                device_id_type=pl.DeviceIdType.MESH,
            ).start()
        pltpu.make_async_copy(corner, corner, corner_send).wait()

    @pl.when(h == 1)
    def _():
        pltpu.make_async_copy(corner_out, corner_out, corner_recv).wait()

    own.wait()
    seven = out.at[pl.ds(0, 7)]
    pltpu.make_async_copy(seven, seven, recv).wait()
    pltpu.make_async_copy(seven, seven, send).wait()


def spread(blocks, corner):
    anywhere = pl.BlockSpec(memory_space=pl.ANY)
    return pl.pallas_call(
        spread_kernel,
        out_shape=(
            jax.ShapeDtypeStruct((8, 256, 512), BF16),
            jax.ShapeDtypeStruct((32, 512), BF16),
        ),
        in_specs=[anywhere] * 2,
        out_specs=(anywhere, anywhere),
        scratch_shapes=[pltpu.SemaphoreType.DMA] * 5,
        compiler_params=pltpu.CompilerParams(has_side_effects=True),
        name="spread",
    )(blocks, corner)


def last_kernel(block, below, corner, order, out):
    m = pl.program_id(0)
    mirrored = lax.axis_index("gy") >= HALF
    here = jnp.dot(block[0], order[...], preferred_element_type=F32).reshape(FR, 8, 512)
    out[...] = here

    @pl.when(mirrored)
    def _():
        low = jnp.dot(below[0], order[...], preferred_element_type=F32).reshape(FR, 8, 512)
        first = lax.broadcasted_iota(jnp.int32, (FR, 8, 512), 1) == 0
        out[...] = jnp.where(first, low, here)

        @pl.when(m == 0)
        def _():
            edge = jnp.dot(corner[...], order[...], preferred_element_type=F32)
            out[:, 0:1, :] = edge.reshape(FR, 1, 512)


def last_step(blocks, corner, order):
    return pl.pallas_call(
        last_kernel,
        grid=(8,),
        out_shape=jax.ShapeDtypeStruct((FR, 64, 512), F32),
        in_specs=[
            pl.BlockSpec((1, 256, 512), lambda m: (m, 0, 0)),
            pl.BlockSpec((1, 256, 512), lambda m: (jnp.maximum(m - 1, 0), 0, 0)),
            pl.BlockSpec((32, 512), lambda m: (0, 0)),
            pl.BlockSpec((512, 512), lambda m: (0, 0)),
        ],
        out_specs=pl.BlockSpec((FR, 8, 512), lambda m: (0, m, 0)),
        compiler_params=pltpu.CompilerParams(vmem_limit_bytes=32 * MIB),
        name="last_step",
    )(blocks, blocks, corner, order)


def shards(charge_field):
    tt, wsum = t_table()
    rows_d, rows_m = row_tables()
    slots = x_transform(charge_field, jnp.asarray(x_tables()))
    rec = lax.all_to_all(slots, ("ta", "gy"), 0, 0)
    rec = rec.reshape(TA, GY, 8 * FT, 128)
    blocks, corner = yt_transform(
        rec, jnp.asarray(tt), jnp.asarray(y_tables()), jnp.asarray(rows_d), jnp.asarray(rows_m), 1.0 / (NX * NY * wsum)
    )
    blocks, corner = spread(blocks, corner)
    return last_step(blocks, corner, jnp.asarray(ky_table()))


def solution(mesh):
    return jax.shard_map(
        shards, mesh=mesh, in_specs=(P("ta", "gy", None),), out_specs=P(None, "gy", "ta"), check_vma=False
    )
```

time: 339 us -> 121 us (0.36)
  the two profiles are of different devices: /device:TPU:1 before, /device:TPU:27 now
where the time goes in v1:
time: 121 us
  Pallas kernels  79.6 us (66%)
  blocking collectives  37.5 us (31%)
  local copies, waits for them, and re-layouts  3.94 us (3%)
    pallas_call x1, Pallas kernels, spread(): pl.pallas_call(spread_kernel, out_shape=(jax.ShapeDtypeStruct((8, 256, 51...  54 us
    all_to_all x1, blocking collectives, shards(): rec = lax.all_to_all(slots, ('ta', 'gy'), 0, 0)  37.5 us
    pallas_call x1, Pallas kernels, yt_transform(): pl.pallas_call(functools.partial(yt_kernel, scale), out_shape=(jax.ShapeD...  11 us
    pallas_call x1, Pallas kernels, x_transform(): pl.pallas_call(x_kernel, grid=(X_STEPS,), out_shape=jax.ShapeDtypeStruct(...  8.09 us
    pallas_call x1, Pallas kernels, last_step(): pl.pallas_call(last_kernel, grid=(8,), out_shape=jax.ShapeDtypeStruct((FR...  6.41 us
    unnamed x8, local copies, waits for them, and re-layouts  3.94 us

profile of v1, /device:TPU:27, one launch (start us, length us, event | category | flops | bytes accessed | tf_op | source)
XLA Modules:
  0.0 121.0 jit_solution(17289523922605145976)
XLA Ops:
  0.0 0.0 copy-start.1
  0.0 1.6 %copy-done.1 = bf16[8,64,2048]{2,1,0:T(8,128)(2,1)S(1)} copy-done((bf16[8,64,2048]{2,1,0:T(8,128)(2,1)S(1)}, bf16[8,64,2048]{2,1,0:T(8,128)(2,1)}, u32[]{:S(2)}) %copy-start.1) | copy-done | bytes 2097176
  1.6 8.1 %x_transform.1 = bf16[128,64,128]{2,1,0:T(8,128)(2,1)S(1)} custom-call(bf16[8,64,2048]{2,1,0:T(8,128)(2,1)S(1)} %copy-done.1, bf16[2,1024,1024]{2,1,0:T(8,128)(2,1)} %constant.12.clone.table), custom_call_target="tpu_custom_call" | custom-call | tf_op jit(solution)/shard_map/x_transform/pallas_call | solution.py:139
  9.7 37.5 %all_to_all.5 = bf16[128,64,128]{2,1,0:T(8,128)(2,1)} all-to-all(bf16[128,64,128]{2,1,0:T(8,128)(2,1)S(1)} %x_transform.1), channel_id=1, replica_groups=mesh['ta'=4,'gy'=32] {'ta','gy'}, dimensions={0} | all-to-all | bytes 4194304 | tf_op jit(solution)/shard_map/all_to_all | solution.py:358
  47.2 11.0 %yt_transform.1 = (bf16[8,256,512]{2,1,0:T(8,128)(2,1)}, bf16[4,32,512]{2,1,0:T(8,128)(2,1)}) custom-call(bf16[4,32,64,128]{3,2,1,0:T(8,128)(2,1)} %bitcast.1, bf16[320,256]{1,0:T(8,128)(2,1)} %constant.13.clone.tt, bf16[3,4,512,256]{3,2,1,0:T(8,128)(2,1)} %constant.14.clone.ty, bf16[256,256]{1,0:T(8,128)(2,1)} %constant.15.clone.rows_d, ...), custom_call_target="tpu_custom_call" | custom-call | tf_op jit(solution)/shard_map/yt_transform/pallas_call | solution.py:234
  58.2 0.0 copy-start.2
  58.2 54.0 %spread.1 = (bf16[8,256,512]{2,1,0:T(8,128)(2,1)}, bf16[32,512]{1,0:T(8,128)(2,1)}) custom-call(bf16[8,256,512]{2,1,0:T(8,128)(2,1)} %get-tuple-element.9.blocks, bf16[4,32,512]{2,1,0:T(8,128)(2,1)} %get-tuple-element.10.corner), custom_call_target="tpu_custom_call" | custom-call | tf_op jit(solution)/shard_map/spread/pallas_call | solution.py:305
  112.2 0.0 copy-done.2
  112.2 0.0 copy-start
  112.3 1.6 %copy-done = bf16[8,256,512]{2,1,0:T(8,128)(2,1)S(1)} copy-done((bf16[8,256,512]{2,1,0:T(8,128)(2,1)S(1)}, bf16[8,256,512]{2,1,0:T(8,128)(2,1)}, u32[]{:S(2)}) %copy-start) | copy-done | bytes 2097176
  113.8 0.0 copy-start.3
  113.8 0.8 copy-done.3
  114.6 6.4 %last_step.1 = f32[32,64,512]{2,1,0:T(8,128)} custom-call(bf16[8,256,512]{2,1,0:T(8,128)(2,1)S(1)} %copy-done, bf16[8,256,512]{2,1,0:T(8,128)(2,1)S(1)} %copy-done, bf16[32,512]{1,0:T(8,128)(2,1)S(1)} %copy-done.3, bf16[512,512]{1,0:T(8,128)(2,1)S(1)} %copy-done.2), custom_call_target="tpu_custom_call" | custom-call | tf_op jit(solution)/shard_map/last_step/pallas_call | solution.py:338
Async XLA Ops:
  0.0 1.6 %copy-start.1 = (bf16[8,64,2048]{2,1,0:T(8,128)(2,1)S(1)}, bf16[8,64,2048]{2,1,0:T(8,128)(2,1)}, u32[]{:S(2)}) copy-start(bf16[8,64,2048]{2,1,0:T(8,128)(2,1)} %field.1) | copy-start | bytes 6291460
  58.2 54.0 %copy-start.2 = (bf16[512,512]{1,0:T(8,128)(2,1)S(1)}, bf16[512,512]{1,0:T(8,128)(2,1)}, u32[]{:S(2)}) copy-start(bf16[512,512]{1,0:T(8,128)(2,1)} %constant.17.clone.order) | copy-start | bytes 1572868
  112.2 1.6 %copy-start = (bf16[8,256,512]{2,1,0:T(8,128)(2,1)S(1)}, bf16[8,256,512]{2,1,0:T(8,128)(2,1)}, u32[]{:S(2)}) copy-start(bf16[8,256,512]{2,1,0:T(8,128)(2,1)} %get-tuple-element.11.block.below) | copy-start | bytes 6291460
  113.8 0.8 copy-start.3

commit v2 on v1

--- a/solution.py
+++ b/solution.py
@@ -25,9 +25,15 @@
     return np.asarray(a).astype(np.float32).astype(ml_dtypes.bfloat16)
 
 
-def device_of(group, part):
+def place(group, part):
     a, h = part % TA, part // TA
-    return a * GY + (group if h == 0 else GY - 1 - group)
+    return a, group if h == 0 else GY - 1 - group
+
+
+def order_of(a, g):
+    y, core = 2 * (a // 2) + g // 16, a % 2
+    z, x = g // 4 % 4, g % 4
+    return ((x + y + z) % 4 * 2 + core) * 16 + 4 * y + x
 
 
 @functools.lru_cache(None)
@@ -37,11 +43,11 @@
         for part in range(8):
             for parity in range(2):
                 base = 64 * group + 8 * part + parity
-                kx[parity, device_of(group, part)] = base + 2 * np.arange(4)
+                kx[parity, order_of(*place(group, part))] = base + 2 * np.arange(4)
     n = np.arange(NX // 2)
     angle = 2 * np.pi * ((kx[..., None] * n) % NX) / NX
     re, im = np.cos(angle), -np.sin(angle)
-    zero = device_of(0, 0)
+    zero = order_of(*place(0, 0))
     im[0, zero, 0] = np.cos(np.pi * n)
     both = np.stack([re, im], axis=2)
     return bf(both.reshape(2, DEV * 8, NX // 2))
@@ -109,58 +115,115 @@
 
 
 NT = (((1,), (1,)), ((), ()))
-X_STEPS = 4
-X_ROWS = DEV * 8 // X_STEPS
-
-
-def x_kernel(field, table, out, even, odd):
-    @pl.when(pl.program_id(0) == 0)
-    def _():
-        for t in range(FT):
-            lo = field[t, :, : NX // 2].astype(F32)
-            hi = field[t, :, NX // 2 :].astype(F32)
-            even[YL * t : YL * (t + 1)] = (lo + hi).astype(BF16)
-            odd[YL * t : YL * (t + 1)] = (lo - hi).astype(BF16)
-
-    for s in range(2):
-        for r in range(0, X_ROWS, 128):
-            rows = slice(r, r + 128)
-            e = lax.dot_general(table[0, rows], even[256 * s : 256 * (s + 1)], NT, preferred_element_type=F32)
-            o = lax.dot_general(table[1, rows], odd[256 * s : 256 * (s + 1)], NT, preferred_element_type=F32)
+MESH = pl.DeviceIdType.MESH
+CHUNKS = 8
+CHUNK = DEV // CHUNKS
+
+
+def fused_kernel(
+    scale, field_in, xt_in, tt_in, ty_in, rd_in, rm_in, out, corner_out,
+    field, xt, tt, ty, rows_d, rows_m, even, odd, slots, rec, u0, u1, u2, u3, power_d, power_m, blocks, corner,
+    load, send, recv, local, send2, recv2, local2, corner_send, corner_recv,
+):
+    a, g = lax.axis_index("ta"), lax.axis_index("gy")
+    me = a * GY + g
+    my_y, my_core, my_z, my_x = 2 * (a // 2) + g // 16, a % 2, g // 4 % 4, g % 4
+
+    loads = [
+        pltpu.make_async_copy(src, dst, load.at[i])
+        for i, (src, dst) in enumerate(
+            ((field_in, field), (xt_in, xt), (tt_in, tt), (ty_in, ty), (rd_in, rows_d), (rm_in, rows_m))
+        )
+    ]
+    for copy in loads:
+        copy.start()
+
+    barrier = pltpu.get_barrier_semaphore()
+
+    def greet(o, carry):
+        peer = (me + o) % DEV
+        pl.semaphore_signal(barrier, inc=1, device_id=(peer // GY, peer % GY), device_id_type=MESH)
+        return carry
+
+    lax.fori_loop(1, DEV, greet, 0)
+
+    loads[0].wait()
+
+    def fold(t, carry):
+        rows = pl.ds(pl.multiple_of(YL * t, YL), YL)
+        lo = field[t, :, : NX // 2].astype(F32)
+        hi = field[t, :, NX // 2 :].astype(F32)
+        even[rows] = (lo + hi).astype(BF16)
+        odd[rows] = (lo - hi).astype(BF16)
+        return carry
+
+    lax.fori_loop(0, FT, fold, 0)
+    loads[1].wait()
+
+    first = (my_x + my_y + my_z) % 4 * 2 + my_core
+
+    def x_step(c, carry):
+        k = (first + c) % CHUNKS
+        rows = pl.ds(pl.multiple_of(128 * k, 128), 128)
+        for s in range(2):
+            e = lax.dot_general(xt[0, rows], even[256 * s : 256 * (s + 1)], NT, preferred_element_type=F32)
+            o = lax.dot_general(xt[1, rows], odd[256 * s : 256 * (s + 1)], NT, preferred_element_type=F32)
             for q in range(2):
                 lanes = slice(128 * q, 128 * (q + 1))
                 one, two = halves(e[:, lanes], o[:, lanes])
                 both = jnp.concatenate([one.reshape(16, 8, 128), two.reshape(16, 8, 128)], axis=1)
                 at = 16 * (2 * s + q)
-                out[r // 8 : r // 8 + 16, at : at + 16] = both.astype(BF16)
-
-
-def x_transform(field, table):
-    return pl.pallas_call(
-        x_kernel,
-        grid=(X_STEPS,),
-        out_shape=jax.ShapeDtypeStruct((DEV, 8 * FT, 128), BF16),
-        in_specs=[
-            pl.BlockSpec((FT, YL, NX), lambda s: (0, 0, 0)),
-            pl.BlockSpec((2, X_ROWS, NX // 2), lambda s: (0, s, 0)),
-        ],
-        out_specs=pl.BlockSpec((DEV // X_STEPS, 8 * FT, 128), lambda s: (s, 0, 0)),
-        scratch_shapes=[pltpu.VMEM((FT * YL, NX // 2), BF16)] * 2,
-        compiler_params=pltpu.CompilerParams(vmem_limit_bytes=48 * MIB),
-        name="x_transform",
-    )(field, table)
-
-
-def yt_kernel(scale, rec, tt, ty, rows_d, rows_m, out, corner, u0, u1, u2, u3, power_d, power_m):
-    special = (lax.axis_index("ta") == 0) & (lax.axis_index("gy") == 0)
+                slots[pl.ds(16 * k, 16), at : at + 16] = both.astype(BF16)
+
+        @pl.when(c == 0)
+        def _():
+            pl.semaphore_wait(barrier, DEV - 1)
+
+        total, core = k // 2, k % 2
+
+        def send_step(i, carry):
+            y, x = (my_y + i // 4) % 4, (my_x + i % 4) % 4
+            z = (total + 8 - x - y) % 4
+            ta, tg = 2 * (y // 2) + core, 16 * (y % 2) + 4 * z + x
+            src = slots.at[16 * k + 4 * y + x]
+            dst = rec.at[me]
+            mine = (ta == a) & (tg == g)
+
+            @pl.when(mine)
+            def _():
+                pltpu.make_async_copy(src, dst, local).start()
+
+            @pl.when(jnp.logical_not(mine))
+            def _():
+                pltpu.make_async_remote_copy(
+                    src_ref=src, dst_ref=dst, send_sem=send, recv_sem=recv, device_id=(ta, tg), device_id_type=MESH
+                ).start()
+
+            return carry
+
+        lax.fori_loop(0, CHUNK, send_step, 0)
+        return carry
+
+    lax.fori_loop(0, CHUNKS, x_step, 0)
+
+    for copy in loads[2:]:
+        copy.wait()
+    pltpu.make_async_copy(slots.at[0], rec.at[0], local).wait()
+    most = rec.at[pl.ds(0, DEV - 1)]
+    pltpu.make_async_copy(most, most, recv).wait()
+
+    special = (a == 0) & (g == 0)
     flag = jnp.where(special, 1.0, 0.0).astype(F32)
+
+    def rec_of(row):
+        return jnp.concatenate([rec[GY * t + row] for t in range(TA)], axis=0)
 
     def time_step(q, carry):
         z = []
         for n in range(4):
             pair = 4 * n + q
-            left = rec[:, 2 * pair].reshape(256, 128)
-            right = rec[:, 2 * pair + 1].reshape(256, 128)
+            left = rec_of(2 * pair)
+            right = rec_of(2 * pair + 1)
             v = jnp.dot(tt[...], jnp.concatenate([left, right], axis=1), preferred_element_type=F32)
             ve, vo = halves(v[:, :128], v[:, 128:])
             re0 = ve[:32] + flag * ve[288:320]
@@ -196,7 +259,7 @@
         re, im = p1 - p4, p3 + p2
         return (re * re + im * im) * scale
 
-    def y_step(a, carry):
+    def y_step(a):
         def put(ref, block, quarter, value):
             lanes = pl.ds(pl.multiple_of(512 * block + 128 * quarter, 128), 128)
             ref[:, lanes] = value.astype(BF16)
@@ -214,66 +277,44 @@
         down = minus(*products(u3, ty[2, a]))
         put(power_m, a, 1, mirrored(down))
         put(power_d, 3 - a, 3, down[:256])
-        return carry
-
-    lax.fori_loop(0, 4, y_step, 0)
-
-    def row_step(a, carry):
-        lanes = pl.ds(pl.multiple_of(512 * a, 512), 512)
-        out[a] = jnp.dot(rows_d[...], power_d[:, lanes], preferred_element_type=F32).astype(BF16)
-        both = jnp.dot(rows_m[...], power_m[:, lanes], preferred_element_type=F32).astype(BF16)
-        out[4 + a] = both[:256]
-        corner[a] = both[256:]
-        return carry
-
-    lax.fori_loop(0, 4, row_step, 0)
-
-
-def yt_transform(rec, tt, ty, rows_d, rows_m, scale):
-    vm = pl.BlockSpec(memory_space=pltpu.VMEM)
-    return pl.pallas_call(
-        functools.partial(yt_kernel, scale),
-        out_shape=(
-            jax.ShapeDtypeStruct((8, 256, 512), BF16),
-            jax.ShapeDtypeStruct((4, 32, 512), BF16),
-        ),
-        in_specs=[vm] * 5,
-        out_specs=(vm, vm),
-        scratch_shapes=[pltpu.VMEM((576, 512), BF16)] * 4 + [pltpu.VMEM((256, 2048), BF16)] * 2,
-        compiler_params=pltpu.CompilerParams(vmem_limit_bytes=56 * MIB),
-        name="yt_transform",
-    )(rec, tt, ty, rows_d, rows_m)
-
-
-def spread_kernel(blocks, corner, out, corner_out, send, recv, local, corner_send, corner_recv):
-    a, g = lax.axis_index("ta"), lax.axis_index("gy")
+
     h = g // HALF
     group = jnp.where(h == 0, g, GY - 1 - g)
     part = a + TA * h
 
-    def target(member):
+    def send_block(member):
         ta, th = member % TA, member // TA
-        return ta, jnp.where(th == 0, group, GY - 1 - group), th
-
-    slot_here = jnp.where(h == 0, part, 7 - part)
-    own = pltpu.make_async_copy(blocks.at[part], out.at[slot_here], local)
-    own.start()
-
-    def send_one(k, carry):
-        member = (part + k) % 8
-        ta, tg, th = target(member)
-        slot = jnp.where(th == 0, part, 7 - part)
-        pltpu.make_async_remote_copy(
-            src_ref=blocks.at[member],
-            dst_ref=out.at[slot],
-            send_sem=send,
-            recv_sem=recv,
-            device_id=(ta, tg),
-            device_id_type=pl.DeviceIdType.MESH,
-        ).start()
+        tg = jnp.where(th == 0, group, GY - 1 - group)
+        src = blocks.at[member]
+        dst = out.at[jnp.where(th == 0, part, 7 - part)]
+
+        @pl.when(member == part)
+        def _():
+            pltpu.make_async_copy(src, dst, local2).start()
+
+        @pl.when(member != part)
+        def _():
+            pltpu.make_async_remote_copy(
+                src_ref=src, dst_ref=dst, send_sem=send2, recv_sem=recv2, device_id=(ta, tg), device_id_type=MESH
+            ).start()
+
+    def row_step(a):
+        lanes = pl.ds(pl.multiple_of(512 * a, 512), 512)
+        both = jnp.dot(rows_m[...], power_m[:, lanes], preferred_element_type=F32).astype(BF16)
+        blocks[4 + a] = both[:256]
+        corner[a] = both[256:]
+        send_block(4 + a)
+        blocks[a] = jnp.dot(rows_d[...], power_d[:, lanes], preferred_element_type=F32).astype(BF16)
+        send_block(a)
+
+    def pair_step(i, carry):
+        y_step(i)
+        y_step(3 - i)
+        row_step(i)
+        row_step(3 - i)
         return carry
 
-    lax.fori_loop(1, 8, send_one, 0)
+    lax.fori_loop(0, 2, pair_step, 0)
     has_corner = part == 0
     corner_to = GY - 1 - (group + HALF - 1) % HALF
 
@@ -281,12 +322,8 @@
     def _():
         for ta in range(TA):
             pltpu.make_async_remote_copy(
-                src_ref=corner.at[ta],
-                dst_ref=corner_out,
-                send_sem=corner_send,
-                recv_sem=corner_recv,
-                device_id=(ta, corner_to),
-                device_id_type=pl.DeviceIdType.MESH,
+                src_ref=corner.at[ta], dst_ref=corner_out, send_sem=corner_send, recv_sem=corner_recv,
+                device_id=(ta, corner_to), device_id_type=MESH,
             ).start()
         pltpu.make_async_copy(corner, corner, corner_send).wait()
 
@@ -294,26 +331,37 @@
     def _():
         pltpu.make_async_copy(corner_out, corner_out, corner_recv).wait()
 
-    own.wait()
+    pltpu.make_async_copy(most, most, send).wait()
+    pltpu.make_async_copy(blocks.at[0], out.at[0], local2).wait()
     seven = out.at[pl.ds(0, 7)]
-    pltpu.make_async_copy(seven, seven, recv).wait()
-    pltpu.make_async_copy(seven, seven, send).wait()
-
-
-def spread(blocks, corner):
+    pltpu.make_async_copy(seven, seven, recv2).wait()
+    pltpu.make_async_copy(seven, seven, send2).wait()
+
+
+def fused(field, xt, tt, ty, rows_d, rows_m, scale):
     anywhere = pl.BlockSpec(memory_space=pl.ANY)
+    operands = (field, xt, tt, ty, rows_d, rows_m)
+    half = (FT * YL, NX // 2)
+    dma = pltpu.SemaphoreType.DMA
     return pl.pallas_call(
-        spread_kernel,
+        functools.partial(fused_kernel, scale),
         out_shape=(
             jax.ShapeDtypeStruct((8, 256, 512), BF16),
             jax.ShapeDtypeStruct((32, 512), BF16),
         ),
-        in_specs=[anywhere] * 2,
+        in_specs=[anywhere] * 6,
         out_specs=(anywhere, anywhere),
-        scratch_shapes=[pltpu.SemaphoreType.DMA] * 5,
-        compiler_params=pltpu.CompilerParams(has_side_effects=True),
-        name="spread",
-    )(blocks, corner)
+        scratch_shapes=[pltpu.VMEM(x.shape, BF16) for x in operands]
+        + [pltpu.VMEM(half, BF16)] * 2
+        + [pltpu.VMEM((DEV, 8 * FT, 128), BF16)] * 2
+        + [pltpu.VMEM((576, 512), BF16)] * 4
+        + [pltpu.VMEM((256, 2048), BF16)] * 2
+        + [pltpu.VMEM((8, 256, 512), BF16), pltpu.VMEM((4, 32, 512), BF16)]
+        + [dma((6,))]
+        + [dma] * 8,
+        compiler_params=pltpu.CompilerParams(collective_id=3, has_side_effects=True, vmem_limit_bytes=56 * MIB),
+        name="fused",
+    )(*operands)
 
 
 def last_kernel(block, below, corner, order, out):
@@ -353,14 +401,8 @@
 
 def shards(charge_field):
     tt, wsum = t_table()
-    rows_d, rows_m = row_tables()
-    slots = x_transform(charge_field, jnp.asarray(x_tables()))
-    rec = lax.all_to_all(slots, ("ta", "gy"), 0, 0)
-    rec = rec.reshape(TA, GY, 8 * FT, 128)
-    blocks, corner = yt_transform(
-        rec, jnp.asarray(tt), jnp.asarray(y_tables()), jnp.asarray(rows_d), jnp.asarray(rows_m), 1.0 / (NX * NY * wsum)
-    )
-    blocks, corner = spread(blocks, corner)
+    tables = [jnp.asarray(x) for x in (x_tables(), tt, y_tables(), *row_tables())]
+    blocks, corner = fused(charge_field, *tables, 1.0 / (NX * NY * wsum))
     return last_step(blocks, corner, jnp.asarray(ky_table()))
 
 

time: 121 us -> 90.3 us (0.75)
  the two profiles are of different devices: /device:TPU:27 before, /device:TPU:26 now
where the time goes in v2:
time: 90.3 us; the launch traced here: 90.1 us
  Pallas kernels  87.8 us (97%)
  local copies, waits for them, and re-layouts  2.35 us (3%)
    pallas_call x1, Pallas kernels, fused(): pl.pallas_call(functools.partial(fused_kernel, scale), out_shape=(jax.Sha...  81.4 us
    pallas_call x1, Pallas kernels, last_step(): pl.pallas_call(last_kernel, grid=(8,), out_shape=jax.ShapeDtypeStruct((FR...  6.41 us
    unnamed x6, local copies, waits for them, and re-layouts  2.35 us

profile of v2, /device:TPU:26, one launch (start us, length us, event | category | flops | bytes accessed | tf_op | source)
XLA Modules:
  0.0 90.1 jit_solution(15597556318058319818)
XLA Ops:
  0.0 0.0 copy-start.1
  0.0 81.4 %fused.1 = (bf16[8,256,512]{2,1,0:T(8,128)(2,1)}, bf16[32,512]{1,0:T(8,128)(2,1)}) custom-call(bf16[8,64,2048]{2,1,0:T(8,128)(2,1)} %field_in.1, bf16[2,1024,1024]{2,1,0:T(8,128)(2,1)} %constant.12.clone.xt_in, bf16[320,256]{1,0:T(8,128)(2,1)} %constant.13.clone.tt_in, bf16[3,4,512,256]{3,2,1,0:T(8,128)(2,1)} %constant.14.clone.ty_in, ...), custom_call_target="tpu_custom_call" | custom-call | tf_op jit(solution)/shard_map/fused/pallas_call | solution.py:346
  81.4 0.0 copy-done.1
  81.4 0.0 copy-start
  81.4 1.6 %copy-done = bf16[8,256,512]{2,1,0:T(8,128)(2,1)S(1)} copy-done((bf16[8,256,512]{2,1,0:T(8,128)(2,1)S(1)}, bf16[8,256,512]{2,1,0:T(8,128)(2,1)}, u32[]{:S(2)}) %copy-start) | copy-done | bytes 2097176
  83.0 0.0 copy-start.2
  83.0 0.8 copy-done.2
  83.7 6.4 %last_step.1 = f32[32,64,512]{2,1,0:T(8,128)} custom-call(bf16[8,256,512]{2,1,0:T(8,128)(2,1)S(1)} %copy-done, bf16[8,256,512]{2,1,0:T(8,128)(2,1)S(1)} %copy-done, bf16[32,512]{1,0:T(8,128)(2,1)S(1)} %copy-done.2, bf16[512,512]{1,0:T(8,128)(2,1)S(1)} %copy-done.1), custom_call_target="tpu_custom_call" | custom-call | tf_op jit(solution)/shard_map/last_step/pallas_call | solution.py:386
Async XLA Ops:
  0.0 81.4 %copy-start.1 = (bf16[512,512]{1,0:T(8,128)(2,1)S(1)}, bf16[512,512]{1,0:T(8,128)(2,1)}, u32[]{:S(2)}) copy-start(bf16[512,512]{1,0:T(8,128)(2,1)} %constant.17.clone.order) | copy-start | bytes 1572868
  81.4 1.6 %copy-start = (bf16[8,256,512]{2,1,0:T(8,128)(2,1)S(1)}, bf16[8,256,512]{2,1,0:T(8,128)(2,1)}, u32[]{:S(2)}) copy-start(bf16[8,256,512]{2,1,0:T(8,128)(2,1)} %get-tuple-element.7.block.below) | copy-start | bytes 6291460
  83.0 0.8 copy-start.2

commit v3 on v2

--- a/solution.py
+++ b/solution.py
@@ -118,27 +118,39 @@
 MESH = pl.DeviceIdType.MESH
 CHUNKS = 8
 CHUNK = DEV // CHUNKS
+PIECE = 64
 
 
 def fused_kernel(
     scale, field_in, xt_in, tt_in, ty_in, rd_in, rm_in, out, corner_out,
     field, xt, tt, ty, rows_d, rows_m, even, odd, slots, rec, u0, u1, u2, u3, power_d, power_m, blocks, corner,
-    load, send, recv, local, send2, recv2, local2, corner_send, corner_recv,
+    frame_load, table_load, load, send, recv, local, send2, recv2, local2, corner_send, corner_recv,
 ):
     a, g = lax.axis_index("ta"), lax.axis_index("gy")
     me = a * GY + g
     my_y, my_core, my_z, my_x = 2 * (a // 2) + g // 16, a % 2, g // 4 % 4, g % 4
 
+    first = (my_x + my_y + my_z) % 4 * 2 + my_core
+    barrier = pltpu.get_barrier_semaphore()
+
+    def frame(t):
+        return pltpu.make_async_copy(field_in.at[t], field.at[t], frame_load.at[t])
+
+    def table(c):
+        rows = pl.ds(pl.multiple_of(128 * ((first + c) % CHUNKS), 128), 128)
+        return pltpu.make_async_copy(xt_in.at[:, rows], xt.at[:, rows], table_load.at[c])
+
     loads = [
         pltpu.make_async_copy(src, dst, load.at[i])
-        for i, (src, dst) in enumerate(
-            ((field_in, field), (xt_in, xt), (tt_in, tt), (ty_in, ty), (rd_in, rows_d), (rm_in, rows_m))
-        )
+        for i, (src, dst) in enumerate(((tt_in, tt), (ty_in, ty), (rd_in, rows_d), (rm_in, rows_m)))
     ]
-    for copy in loads:
-        copy.start()
-
-    barrier = pltpu.get_barrier_semaphore()
+
+    def start_frame(t, carry):
+        frame(t).start()
+        return carry
+
+    lax.fori_loop(0, FT, start_frame, 0)
+    table(0).start()
 
     def greet(o, carry):
         peer = (me + o) % DEV
@@ -147,9 +159,14 @@
 
     lax.fori_loop(1, DEV, greet, 0)
 
-    loads[0].wait()
+    def start_table(c, carry):
+        table(c).start()
+        return carry
+
+    lax.fori_loop(1, CHUNKS, start_table, 0)
 
     def fold(t, carry):
+        frame(t).wait()
         rows = pl.ds(pl.multiple_of(YL * t, YL), YL)
         lo = field[t, :, : NX // 2].astype(F32)
         hi = field[t, :, NX // 2 :].astype(F32)
@@ -158,11 +175,11 @@
         return carry
 
     lax.fori_loop(0, FT, fold, 0)
-    loads[1].wait()
-
-    first = (my_x + my_y + my_z) % 4 * 2 + my_core
+    for copy in loads:
+        copy.start()
 
     def x_step(c, carry):
+        table(c).wait()
         k = (first + c) % CHUNKS
         rows = pl.ds(pl.multiple_of(128 * k, 128), 128)
         for s in range(2):
@@ -206,7 +223,7 @@
 
     lax.fori_loop(0, CHUNKS, x_step, 0)
 
-    for copy in loads[2:]:
+    for copy in loads:
         copy.wait()
     pltpu.make_async_copy(slots.at[0], rec.at[0], local).wait()
     most = rec.at[pl.ds(0, DEV - 1)]
@@ -259,18 +276,14 @@
         re, im = p1 - p4, p3 + p2
         return (re * re + im * im) * scale
 
-    def y_step(a):
-        def put(ref, block, quarter, value):
-            lanes = pl.ds(pl.multiple_of(512 * block + 128 * quarter, 128), 128)
-            ref[:, lanes] = value.astype(BF16)
-
-        def mirrored(value):
-            return jnp.concatenate([jnp.where(special, value[256:], value[:32]), value[32:256]], axis=0)
-
-        for c, ref in ((0, u0), (2, u2)):
-            parts = products(ref, ty[c // 2, a])
-            put(power_d, a, c, plus(*parts)[:256])
-            put(power_m, a, c, mirrored(minus(*parts)))
+    def put(ref, block, quarter, value):
+        lanes = pl.ds(pl.multiple_of(512 * block + 128 * quarter, 128), 128)
+        ref[:, lanes] = value.astype(BF16)
+
+    def mirrored(value):
+        return jnp.concatenate([jnp.where(special, value[256:], value[:32]), value[32:256]], axis=0)
+
+    def odd_step(a):
         up = plus(*products(u1, ty[2, a]))
         put(power_d, a, 1, up[:256])
         put(power_m, 3 - a, 3, mirrored(up))
@@ -278,15 +291,22 @@
         put(power_m, a, 1, mirrored(down))
         put(power_d, 3 - a, 3, down[:256])
 
+    def even_step(a):
+        for c, ref in ((0, u0), (2, u2)):
+            parts = products(ref, ty[c // 2, a])
+            put(power_d, a, c, plus(*parts)[:256])
+            put(power_m, a, c, mirrored(minus(*parts)))
+
     h = g // HALF
     group = jnp.where(h == 0, g, GY - 1 - g)
     part = a + TA * h
 
-    def send_block(member):
+    def send_piece(member, piece):
         ta, th = member % TA, member // TA
         tg = jnp.where(th == 0, group, GY - 1 - group)
-        src = blocks.at[member]
-        dst = out.at[jnp.where(th == 0, part, 7 - part)]
+        rows = pl.ds(pl.multiple_of(PIECE * piece, PIECE), PIECE)
+        src = blocks.at[member, rows]
+        dst = out.at[jnp.where(th == 0, part, 7 - part), rows]
 
         @pl.when(member == part)
         def _():
@@ -303,15 +323,23 @@
         both = jnp.dot(rows_m[...], power_m[:, lanes], preferred_element_type=F32).astype(BF16)
         blocks[4 + a] = both[:256]
         corner[a] = both[256:]
-        send_block(4 + a)
         blocks[a] = jnp.dot(rows_d[...], power_d[:, lanes], preferred_element_type=F32).astype(BF16)
-        send_block(a)
 
     def pair_step(i, carry):
-        y_step(i)
-        y_step(3 - i)
-        row_step(i)
-        row_step(3 - i)
+        low = (i + my_core) % 2
+        far = jnp.where(a // 2 == 0, 3 - low, low)
+        odd_step(far)
+        odd_step(3 - far)
+        for to in (far, 3 - far):
+            even_step(to)
+            row_step(to)
+
+        def pieces(n, carry):
+            to = jnp.where(n % 4 < 2, far, 3 - far)
+            send_piece(to + TA * ((n + 1) % 2), n // 4)
+            return carry
+
+        lax.fori_loop(0, 4 * (256 // PIECE), pieces, 0)
         return carry
 
     lax.fori_loop(0, 2, pair_step, 0)
@@ -357,46 +385,42 @@
         + [pltpu.VMEM((576, 512), BF16)] * 4
         + [pltpu.VMEM((256, 2048), BF16)] * 2
         + [pltpu.VMEM((8, 256, 512), BF16), pltpu.VMEM((4, 32, 512), BF16)]
-        + [dma((6,))]
+        + [dma((FT,)), dma((CHUNKS,)), dma((4,))]
         + [dma] * 8,
         compiler_params=pltpu.CompilerParams(collective_id=3, has_side_effects=True, vmem_limit_bytes=56 * MIB),
         name="fused",
     )(*operands)
 
 
-def last_kernel(block, below, corner, order, out):
-    m = pl.program_id(0)
+LAST_STEPS = 2
+LAST = FR // LAST_STEPS
+
+
+def last_kernel(blocks, corner, order, out):
     mirrored = lax.axis_index("gy") >= HALF
-    here = jnp.dot(block[0], order[...], preferred_element_type=F32).reshape(FR, 8, 512)
-    out[...] = here
-
-    @pl.when(mirrored)
-    def _():
-        low = jnp.dot(below[0], order[...], preferred_element_type=F32).reshape(FR, 8, 512)
-        first = lax.broadcasted_iota(jnp.int32, (FR, 8, 512), 1) == 0
-        out[...] = jnp.where(first, low, here)
-
-        @pl.when(m == 0)
-        def _():
-            edge = jnp.dot(corner[...], order[...], preferred_element_type=F32)
-            out[:, 0:1, :] = edge.reshape(FR, 1, 512)
+    first = (lax.broadcasted_iota(jnp.int32, (LAST, 8, 512), 1) == 0) & mirrored
+    edge = jnp.dot(corner[...], order[...], preferred_element_type=F32)
+    below = jnp.broadcast_to(edge.reshape(LAST, 1, 512), (LAST, 8, 512))
+    for m in range(8):
+        here = jnp.dot(blocks[m], order[...], preferred_element_type=F32).reshape(LAST, 8, 512)
+        out[:, 8 * m : 8 * m + 8] = jnp.where(first, below, here)
+        below = here
 
 
 def last_step(blocks, corner, order):
     return pl.pallas_call(
         last_kernel,
-        grid=(8,),
+        grid=(LAST_STEPS,),
         out_shape=jax.ShapeDtypeStruct((FR, 64, 512), F32),
         in_specs=[
-            pl.BlockSpec((1, 256, 512), lambda m: (m, 0, 0)),
-            pl.BlockSpec((1, 256, 512), lambda m: (jnp.maximum(m - 1, 0), 0, 0)),
-            pl.BlockSpec((32, 512), lambda m: (0, 0)),
+            pl.BlockSpec((8, LAST * 8, 512), lambda m: (0, m, 0)),
+            pl.BlockSpec((LAST, 512), lambda m: (m, 0)),
             pl.BlockSpec((512, 512), lambda m: (0, 0)),
         ],
-        out_specs=pl.BlockSpec((FR, 8, 512), lambda m: (0, m, 0)),
-        compiler_params=pltpu.CompilerParams(vmem_limit_bytes=32 * MIB),
+        out_specs=pl.BlockSpec((LAST, 64, 512), lambda m: (m, 0, 0)),
+        compiler_params=pltpu.CompilerParams(vmem_limit_bytes=62 * MIB),
         name="last_step",
-    )(blocks, blocks, corner, order)
+    )(blocks, corner, order)
 
 
 def shards(charge_field):

time: 90.3 us -> 75 us (0.83)
  the two profiles are of different devices: /device:TPU:26 before, /device:TPU:1 now
where the time goes in v3:
time: 75 us; the launch traced here: 74.8 us
  Pallas kernels  74.8 us (100%)
    pallas_call x1, Pallas kernels, fused(): pl.pallas_call(functools.partial(fused_kernel, scale), out_shape=(jax.Sha...  70.5 us
    pallas_call x1, Pallas kernels, last_step(): pl.pallas_call(last_kernel, grid=(LAST_STEPS,), out_shape=jax.ShapeDtypeS...  4.31 us

profile of v3, /device:TPU:1, one launch (start us, length us, event | category | flops | bytes accessed | tf_op | source)
XLA Modules:
  0.0 74.8 jit_solution(6691746730398471226)
XLA Ops:
  0.0 70.5 %fused.1 = (bf16[8,256,512]{2,1,0:T(8,128)(2,1)}, bf16[32,512]{1,0:T(8,128)(2,1)}) custom-call(bf16[8,64,2048]{2,1,0:T(8,128)(2,1)} %field_in.1, bf16[2,1024,1024]{2,1,0:T(8,128)(2,1)} %constant.12.clone.xt_in, bf16[320,256]{1,0:T(8,128)(2,1)} %constant.13.clone.tt_in, bf16[3,4,512,256]{3,2,1,0:T(8,128)(2,1)} %constant.14.clone.ty_in, ...), custom_call_target="tpu_custom_call" | custom-call | tf_op jit(solution)/shard_map/fused/pallas_call | solution.py:374
  70.5 4.3 %last_step.1 = f32[32,64,512]{2,1,0:T(8,128)} custom-call(bf16[8,256,512]{2,1,0:T(8,128)(2,1)} %get-tuple-element.7.blocks, bf16[32,512]{1,0:T(8,128)(2,1)} %get-tuple-element.8.corner, bf16[512,512]{1,0:T(8,128)(2,1)} %constant.17.clone.order), custom_call_target="tpu_custom_call" | custom-call | tf_op jit(solution)/shard_map/last_step/pallas_call | solution.py:411

commit v4 on v3

v4 whole, which is shorter than its diff:
```python
import functools
import math

import jax
import jax.numpy as jnp
import ml_dtypes
import numpy as np
from jax import lax
from jax.experimental import pallas as pl
from jax.experimental.pallas import tpu as pltpu
from jax.sharding import PartitionSpec as P

FR, NX, NY = 32, 2048, 2048
TA, GY = 4, 32
DEV = TA * GY
FT = FR // TA
YL = NY // GY
SLOT = 8
HALF = GY // 2
F32, BF16 = jnp.float32, jnp.bfloat16
MIB = 1 << 20


def bf(a):
    return np.asarray(a).astype(np.float32).astype(ml_dtypes.bfloat16)


def place(group, part):
    a, h = part % TA, part // TA
    return a, group if h == 0 else GY - 1 - group


def order_of(a, g):
    y, core = 2 * (a // 2) + g // 16, a % 2
    z, x = g // 4 % 4, g % 4
    return ((x + y + z) % 4 * 2 + core) * 16 + 4 * y + x


@functools.lru_cache(None)
def x_tables():
    kx = np.zeros((2, DEV, 4), np.int64)
    for group in range(HALF):
        for part in range(8):
            for parity in range(2):
                base = 64 * group + 8 * part + parity
                kx[parity, order_of(*place(group, part))] = base + 2 * np.arange(4)
    n = np.arange(NX // 2)
    angle = 2 * np.pi * ((kx[..., None] * n) % NX) / NX
    re, im = np.cos(angle), -np.sin(angle)
    zero = order_of(*place(0, 0))
    im[0, zero, 0] = np.cos(np.pi * n)
    both = np.stack([re, im], axis=2)
    return bf(both.reshape(2, DEV * 8, NX // 2))


@functools.lru_cache(None)
def t_table():
    t = np.arange(FR)
    window = 0.5 - 0.5 * np.cos(2 * np.pi * (t + 0.5) / FR)
    angle = 2 * np.pi * ((t[:, None] * t[None, :]) % FR) / FR
    out = np.zeros((2, 4, FR, FR, 4))
    for p in range(4):
        out[0, p, :, :, p] = np.cos(angle) * window
        out[1, p, :, :, p] = np.sin(angle) * window
    return bf(out.reshape(2 * 4 * FR, FR * 4)), float(np.sum(window * window))


@functools.lru_cache(None)
def y_tables():
    n, k = np.arange(NY // 4), np.arange(NY // 4)
    out = []
    for q in (0, 2, 1):
        angle = 2 * np.pi * ((n[:, None] * (4 * k[None, :] + q)) % NY) / NY
        cs = np.stack([np.cos(angle).reshape(-1, 4, 128), np.sin(angle).reshape(-1, 4, 128)], axis=2)
        out.append(cs.transpose(1, 0, 2, 3).reshape(4, NY // 4, 256))
    return bf(np.stack(out))


@functools.lru_cache(None)
def row_tables():
    out = np.zeros((2, FR, 8, 2, 4, FR))
    for w in range(FR):
        for j in range(8):
            out[0, w, j, j % 2, j // 2, w] = 1
            out[1, w, (8 - j) % 8, j % 2, j // 2, -w % FR] = 1
    return bf(out.reshape(2, FR * 8, FR * 8))


@functools.lru_cache(None)
def ky_table():
    out = np.zeros((4, 128, 128, 4))
    k = np.arange(128)
    for q in range(3):
        out[q, k, k, q] = 1
    out[3, k, 127 - k, 3] = 1
    return bf(out.reshape(512, 512))


def halves(first, second):
    low = lax.broadcasted_iota(jnp.int32, first.shape, first.ndim - 1) < 64
    one = jnp.where(low, first, pltpu.roll(second, 64, first.ndim - 1))
    two = jnp.where(low, pltpu.roll(first, 64, first.ndim - 1), second)
    return one, two


NT = (((1,), (1,)), ((), ()))
MESH = pl.DeviceIdType.MESH
CHUNKS = 8
CHUNK = DEV // CHUNKS
PIECES = 128, 64


def fused_kernel(
    scale, field_in, xt_in, tt_in, ty_in, out, corner_out,
    field, xt, tt, ty, folded, slots, rec, u0, u1, u2, u3, blocks,
    frame_load, table_load, load, send, recv, local, send2, recv2, local2, corner_send, corner_recv,
):
    a, g = lax.axis_index("ta"), lax.axis_index("gy")
    me = a * GY + g
    my_y, my_core, my_z, my_x = 2 * (a >> 1) + (g >> 4), a & 1, (g >> 2) & 3, g & 3
    first = ((my_x + my_y + my_z) & 3) * 2 + my_core
    barrier = pltpu.get_barrier_semaphore()

    def frame(t):
        return pltpu.make_async_copy(field_in.at[t], field.at[t], frame_load.at[t])

    def table(s, c):
        rows = pl.ds(pl.multiple_of(128 * ((first + c) & 7), 128), 128)
        return pltpu.make_async_copy(xt_in.at[s, rows], xt.at[s, rows], table_load.at[s, c])

    loads = [pltpu.make_async_copy(src, dst, load.at[i]) for i, (src, dst) in enumerate(((tt_in, tt), (ty_in, ty)))]

    for t in range(FT):
        frame(t).start()
    table(0, 0).start()

    for t in range(FT):
        for o in range(max(16 * t, 1), 16 * (t + 1)):
            peer = (me + o) & (DEV - 1)
            pl.semaphore_signal(barrier, inc=1, device_id=(peer >> 5, peer & 31), device_id_type=MESH)
        frame(t).wait()
        rows = slice(YL * t, YL * (t + 1))
        lo = field[t, :, : NX // 2].astype(F32)
        hi = field[t, :, NX // 2 :].astype(F32)
        folded[0, rows] = (lo + hi).astype(BF16)
        folded[1, rows] = (lo - hi).astype(BF16)

    for s in range(2):

        def start_table(c, carry):
            table(s, c).start()
            return carry

        lax.fori_loop(1 - s, CHUNKS, start_table, 0)
    for copy in loads:
        copy.start()

    def x_step(s, c):
        table(s, c).wait()
        k = (first + c) & 7
        rows = pl.ds(pl.multiple_of(128 * k, 128), 128)
        tile = (16, 8, 128)
        stay = (lax.broadcasted_iota(jnp.int32, tile, 1) < 4) == (lax.broadcasted_iota(jnp.int32, tile, 2) < 64)
        for n in range(2):
            both = lax.dot_general(
                xt[s, rows], folded[s, 256 * n : 256 * (n + 1)], NT, preferred_element_type=F32
            )
            parts = []
            for q in range(2):
                part = both[:, 128 * q : 128 * (q + 1)].reshape(tile)
                parts.append(jnp.where(stay, part, pltpu.roll(pltpu.roll(part, 64, 2), 4, 1)))
            slots[s, pl.ds(16 * k, 16), 16 * n : 16 * (n + 1)] = jnp.concatenate(parts, axis=1).astype(BF16)

        if s == 0:

            @pl.when(c == 0)
            def _():
                pl.semaphore_wait(barrier, DEV - 1)

        total, core = k >> 1, k & 1

        def send_step(i, carry):
            y, x = (my_y + (i >> 2)) & 3, (my_x + i) & 3
            z = (total + 8 - x - y) & 3
            ta, tg = 2 * (y >> 1) + core, 16 * (y & 1) + 4 * z + x
            src = slots.at[s, 16 * k + 4 * y + x]
            dst = rec.at[s, me]
            mine = (ta == a) & (tg == g)

            @pl.when(mine)
            def _():
                pltpu.make_async_copy(src, dst, local.at[s]).start()

            @pl.when(jnp.logical_not(mine))
            def _():
                pltpu.make_async_remote_copy(
                    src_ref=src, dst_ref=dst, send_sem=send, recv_sem=recv.at[s], device_id=(ta, tg), device_id_type=MESH
                ).start()

            return carry

        lax.fori_loop(0, CHUNK, send_step, 0)

    for s in range(2):

        def step(c, carry):
            x_step(s, c)
            return carry

        lax.fori_loop(0, CHUNKS, step, 0)

    for copy in loads:
        copy.wait()

    special = (a == 0) & (g == 0)
    keep = jnp.where(special, 0.0, 1.0).astype(F32)
    h = g >> 4
    group = jnp.where(h == 0, g, GY - 1 - g)
    part = a + TA * h

    def send_piece(s, member, piece, size):
        ta, th = member & 3, member >> 2
        tg = jnp.where(th == 0, group, GY - 1 - group)
        rows = pl.ds(pl.multiple_of(size * piece, size), size)
        to_rows = pl.ds(pl.multiple_of(128 * s + size * piece, size), size)
        src = blocks.at[s, member, rows]
        dst = out.at[jnp.where(th == 0, part, 7 - part), to_rows]

        @pl.when(member == part)
        def _():
            pltpu.make_async_copy(src, dst, local2).start()

        @pl.when(member != part)
        def _():
            pltpu.make_async_remote_copy(
                src_ref=src, dst_ref=dst, send_sem=send2, recv_sem=recv2, device_id=(ta, tg), device_id_type=MESH
            ).start()

    def plus(p1, p2, p3, p4):
        re, im = p1 + p4, p3 - p2
        return (re * re + im * im) * scale

    def minus(p1, p2, p3, p4):
        re, im = p1 - p4, p3 + p2
        return (re * re + im * im) * scale

    most = rec.at[0, pl.ds(0, DEV - 1)]
    corner_to = GY - 1 - ((group + HALF - 1) & (HALF - 1))

    for s in range(2):
        count = 160 if s == 0 else 128
        size = PIECES[s]
        pltpu.make_async_copy(slots.at[s, 0], rec.at[s, 0], local.at[s]).wait()
        pltpu.make_async_copy(most, most, recv.at[s]).wait()

        def rec_of(row):
            return jnp.concatenate([rec[s, GY * t + row] for t in range(TA)], axis=0)

        def time_step(q, carry):
            z = []
            for n in range(4):
                pair = 4 * n + q
                x = jnp.concatenate([rec_of(2 * pair), rec_of(2 * pair + 1)], axis=1)
                v = jnp.dot(tt[...], x, preferred_element_type=F32)
                cr, ci = halves(v[:128, :128], v[:128, 128:])
                sr, si = halves(v[128:, :128], v[128:, 128:])
                if s == 0:
                    re = jnp.concatenate([cr[:32] + keep * si[:32], cr[32:] + si[32:], ci[:32]], axis=0)
                    im = jnp.concatenate([keep * ci[:32] - sr[:32], ci[32:] - sr[32:], -si[:32]], axis=0)
                else:
                    re, im = cr + si, ci - sr
                z.append((re, im))
            (ar, ai), (br, bi), (cr, ci), (dr, di) = z
            sr, si, tr, ti = ar + cr, ai + ci, br + dr, bi + di
            er, ei, fr, fi = ar - cr, ai - ci, br - dr, bi - di
            lanes = pl.ds(pl.multiple_of(128 * q, 128), 128)
            for ref, re, im in (
                (u0, sr + tr, si + ti),
                (u1, er + fi, ei - fr),
                (u2, sr - tr, si - ti),
                (u3, er - fi, ei + fr),
            ):
                ref[:count, lanes] = re.astype(BF16)
                ref[count : 2 * count, lanes] = im.astype(BF16)
            return carry

        lax.fori_loop(0, 4, time_step, 0)

        def products(ref, table):
            both = jnp.dot(ref[: 2 * count], table, preferred_element_type=F32)
            return both[:count, :128], both[:count, 128:], both[count:, :128], both[count:, 128:]

        def put(member, quarter, value):
            blocks[s, member, :, 128 * quarter : 128 * (quarter + 1)] = value.astype(BF16)

        def mirrored(value):
            if s == 1:
                return value
            return jnp.concatenate([jnp.where(special, value[128:], value[:32]), value[32:128]], axis=0)

        def odd_step(b):
            up = plus(*products(u1, ty[2, b]))
            put(b, 1, up[:128])
            put(7 - b, 3, mirrored(up))
            down = minus(*products(u3, ty[2, b]))
            put(4 + b, 1, mirrored(down))
            put(3 - b, 3, down[:128])

        def even_step(b):
            for c, ref in ((0, u0), (2, u2)):
                parts = products(ref, ty[c // 2, b])
                put(b, c, plus(*parts)[:128])
                put(4 + b, c, mirrored(minus(*parts)))

        def pair_step(i, carry):
            low = (i + my_core) & 1
            far = jnp.where(a >> 1 == 0, 3 - low, low)
            for b in (far, 3 - far):
                odd_step(b)
                even_step(b)

            def pieces(n, carry):
                to = jnp.where(n & 3 < 2, far, 3 - far)
                send_piece(s, to + TA * ((n + 1) & 1), n >> 2, size)
                return carry

            lax.fori_loop(0, 4 * (128 // size), pieces, 0)
            return carry

        lax.fori_loop(0, 2, pair_step, 0)
        if s == 0:

            @pl.when(part == 0)
            def _():
                for ta in range(TA):
                    pltpu.make_async_remote_copy(
                        src_ref=blocks.at[0, 4 + ta, pl.ds(0, FR)], dst_ref=corner_out,
                        send_sem=corner_send, recv_sem=corner_recv, device_id=(ta, corner_to), device_id_type=MESH,
                    ).start()

    @pl.when(part == 0)
    def _():
        all_corners = blocks.at[0, 0]
        pltpu.make_async_copy(all_corners, all_corners, corner_send).wait()

    @pl.when(h == 1)
    def _():
        pltpu.make_async_copy(corner_out, corner_out, corner_recv).wait()

    for s in range(2):
        pltpu.make_async_copy(most, most, send).wait()
    pltpu.make_async_copy(out.at[0], out.at[0], local2).wait()
    seven = out.at[pl.ds(0, 7)]
    pltpu.make_async_copy(seven, seven, recv2).wait()
    pltpu.make_async_copy(seven, seven, send2).wait()


def fused(field, xt, tt, ty, scale):
    anywhere = pl.BlockSpec(memory_space=pl.ANY)
    operands = (field, xt, tt, ty)
    dma = pltpu.SemaphoreType.DMA
    return pl.pallas_call(
        functools.partial(fused_kernel, scale),
        out_shape=(
            jax.ShapeDtypeStruct((8, 256, 512), BF16),
            jax.ShapeDtypeStruct((FR, 512), BF16),
        ),
        in_specs=[anywhere] * 4,
        out_specs=(anywhere, anywhere),
        scratch_shapes=[pltpu.VMEM(x.shape, BF16) for x in operands]
        + [pltpu.VMEM((2, FT * YL, NX // 2), BF16)]
        + [pltpu.VMEM((2, DEV, 4 * FT, 128), BF16)] * 2
        + [pltpu.VMEM((320, 512), BF16)] * 4
        + [pltpu.VMEM((2, 8, 128, 512), BF16)]
        + [dma((FT,)), dma((2, CHUNKS)), dma((2,)), dma, dma((2,)), dma((2,))]
        + [dma] * 5,
        compiler_params=pltpu.CompilerParams(collective_id=3, has_side_effects=True, vmem_limit_bytes=56 * MIB),
        name="fused",
    )(*operands)


LAST_STEPS = 2
LAST = 8 // LAST_STEPS


def last_kernel(blocks, corner, rows, order, out, turned, below):
    mirrored = lax.axis_index("gy") >= HALF
    rows_here = rows[jnp.where(mirrored, 1, 0)]
    first = (lax.broadcasted_iota(jnp.int32, (8 * FR, 512), 0) % 8 == 0) & mirrored

    @pl.when(pl.program_id(0) == 0)
    def _():
        edge = jnp.concatenate([corner[...], jnp.zeros((7 * FR, 512), BF16)], axis=0)
        below[...] = jnp.dot(rows_here, edge, preferred_element_type=F32)

    for m in range(LAST):
        here = jnp.dot(rows_here, blocks[m], preferred_element_type=F32)
        turned[m] = jnp.where(first, below[...], here).astype(BF16)
        below[...] = here
    for n in range(2):
        lanes = slice(256 * n, 256 * (n + 1))
        all_rows = turned[...].reshape(LAST * 8 * FR, 512)
        done = jnp.dot(all_rows, order[:, lanes], preferred_element_type=F32).reshape(LAST, FR, 8, 256)
        for m in range(LAST):
            out[:, 8 * m : 8 * m + 8, lanes] = done[m]


def last_step(blocks, corner, rows, order):
    return pl.pallas_call(
        last_kernel,
        grid=(LAST_STEPS,),
        out_shape=jax.ShapeDtypeStruct((FR, 64, 512), F32),
        in_specs=[
            pl.BlockSpec((LAST, 256, 512), lambda m: (m, 0, 0)),
            pl.BlockSpec((FR, 512), lambda m: (0, 0)),
            pl.BlockSpec((2, 256, 256), lambda m: (0, 0, 0)),
            pl.BlockSpec((512, 512), lambda m: (0, 0)),
        ],
        out_specs=pl.BlockSpec((FR, 8 * LAST, 512), lambda m: (0, m, 0)),
        scratch_shapes=[pltpu.VMEM((LAST, 8 * FR, 512), BF16), pltpu.VMEM((8 * FR, 512), F32)],
        compiler_params=pltpu.CompilerParams(vmem_limit_bytes=62 * MIB),
        name="last_step",
    )(blocks, corner, rows, order)


def shards(charge_field):
    tt, wsum = t_table()
    tables = [jnp.asarray(x) for x in (x_tables(), tt, y_tables())]
    blocks, corner = fused(charge_field, *tables, 1.0 / (NX * NY * wsum))
    return last_step(blocks, corner, jnp.asarray(row_tables()), jnp.asarray(ky_table()))


def solution(mesh):
    return jax.shard_map(
        shards, mesh=mesh, in_specs=(P("ta", "gy", None),), out_specs=P(None, "gy", "ta"), check_vma=False
    )
```

time: 75 us -> 67.8 us (0.904)
  the two profiles are of different devices: /device:TPU:1 before, /device:TPU:20 now
where the time goes in v4:
time: 67.8 us; the launch traced here: 67.7 us
  Pallas kernels  67.7 us (100%)
    pallas_call x1, Pallas kernels, fused(): pl.pallas_call(functools.partial(fused_kernel, scale), out_shape=(jax.Sha...  62.6 us
    pallas_call x1, Pallas kernels, last_step(): pl.pallas_call(last_kernel, grid=(LAST_STEPS,), out_shape=jax.ShapeDtypeS...  5.05 us

profile of v4, /device:TPU:20, one launch (start us, length us, event | category | flops | bytes accessed | tf_op | source)
XLA Modules:
  0.0 67.7 jit_solution(16302396928898515814)
XLA Ops:
  0.0 62.6 %fused.1 = (bf16[8,256,512]{2,1,0:T(8,128)(2,1)}, bf16[32,512]{1,0:T(8,128)(2,1)}) custom-call(bf16[8,64,2048]{2,1,0:T(8,128)(2,1)} %field_in.1, bf16[2,1024,1024]{2,1,0:T(8,128)(2,1)} %constant.10.clone.xt_in, bf16[256,128]{1,0:T(8,128)(2,1)} %constant.11.clone.tt_in, bf16[3,4,512,256]{3,2,1,0:T(8,128)(2,1)} %constant.12.clone.ty_in), custom_call_target="tpu_custom_call" | custom-call | tf_op jit(solution)/shard_map/fused/pallas_call | solution.py:362
  62.6 5.0 %last_step.1 = f32[32,64,512]{2,1,0:T(8,128)} custom-call(bf16[8,256,512]{2,1,0:T(8,128)(2,1)} %get-tuple-element.7.blocks, bf16[32,512]{1,0:T(8,128)(2,1)} %get-tuple-element.8.corner, bf16[2,256,256]{2,1,0:T(8,128)(2,1)} %constant.13.clone.rows, bf16[512,512]{1,0:T(8,128)(2,1)} %constant.14.clone.order), custom_call_target="tpu_custom_call" | custom-call | tf_op jit(solution)/shard_map/last_step/pallas_call | solution.py:409

commit v5 on v4

--- a/solution.py
+++ b/solution.py
@@ -133,27 +133,19 @@
     for t in range(FT):
         frame(t).start()
     table(0, 0).start()
+    table(0, 1).start()
+
+    for o in range(1, DEV):
+        peer = (me + o) & (DEV - 1)
+        pl.semaphore_signal(barrier, inc=1, device_id=(peer >> 5, peer & 31), device_id_type=MESH)
 
     for t in range(FT):
-        for o in range(max(16 * t, 1), 16 * (t + 1)):
-            peer = (me + o) & (DEV - 1)
-            pl.semaphore_signal(barrier, inc=1, device_id=(peer >> 5, peer & 31), device_id_type=MESH)
         frame(t).wait()
         rows = slice(YL * t, YL * (t + 1))
         lo = field[t, :, : NX // 2].astype(F32)
         hi = field[t, :, NX // 2 :].astype(F32)
         folded[0, rows] = (lo + hi).astype(BF16)
         folded[1, rows] = (lo - hi).astype(BF16)
-
-    for s in range(2):
-
-        def start_table(c, carry):
-            table(s, c).start()
-            return carry
-
-        lax.fori_loop(1 - s, CHUNKS, start_table, 0)
-    for copy in loads:
-        copy.start()
 
     def x_step(s, c):
         table(s, c).wait()
@@ -171,43 +163,46 @@
                 parts.append(jnp.where(stay, part, pltpu.roll(pltpu.roll(part, 64, 2), 4, 1)))
             slots[s, pl.ds(16 * k, 16), 16 * n : 16 * (n + 1)] = jnp.concatenate(parts, axis=1).astype(BF16)
 
-        if s == 0:
-
-            @pl.when(c == 0)
-            def _():
-                pl.semaphore_wait(barrier, DEV - 1)
-
+    def send_step(s, c):
+        k = (first + c) & 7
         total, core = k >> 1, k & 1
-
-        def send_step(i, carry):
+        for i in range(CHUNK):
             y, x = (my_y + (i >> 2)) & 3, (my_x + i) & 3
             z = (total + 8 - x - y) & 3
-            ta, tg = 2 * (y >> 1) + core, 16 * (y & 1) + 4 * z + x
             src = slots.at[s, 16 * k + 4 * y + x]
             dst = rec.at[s, me]
-            mine = (ta == a) & (tg == g)
-
-            @pl.when(mine)
-            def _():
+            if i == 0 and isinstance(c, int) and c == 0:
                 pltpu.make_async_copy(src, dst, local.at[s]).start()
-
-            @pl.when(jnp.logical_not(mine))
-            def _():
-                pltpu.make_async_remote_copy(
-                    src_ref=src, dst_ref=dst, send_sem=send, recv_sem=recv.at[s], device_id=(ta, tg), device_id_type=MESH
-                ).start()
-
-            return carry
-
-        lax.fori_loop(0, CHUNK, send_step, 0)
+                continue
+            pltpu.make_async_remote_copy(
+                src_ref=src, dst_ref=dst, send_sem=send, recv_sem=recv.at[s],
+                device_id=(2 * (y >> 1) + core, 16 * (y & 1) + 4 * z + x), device_id_type=MESH,
+            ).start()
 
     for s in range(2):
+        x_step(s, 0)
+        if s == 0:
+            pl.semaphore_wait(barrier, DEV - 1)
+        else:
+            send_step(0, CHUNKS - 1)
+        send_step(s, 0)
+        if s == 0:
+            for c in range(2, CHUNKS):
+                table(0, c).start()
+            for c in range(CHUNKS):
+                table(1, c).start()
+        x_step(s, 1)
 
         def step(c, carry):
+            send_step(s, c - 1)
             x_step(s, c)
             return carry
 
-        lax.fori_loop(0, CHUNKS, step, 0)
+        lax.fori_loop(2, CHUNKS, step, 0)
+        if s == 0:
+            for copy in loads:
+                copy.start()
+    send_step(1, CHUNKS - 1)
 
     for copy in loads:
         copy.wait()
@@ -320,7 +315,7 @@
                 even_step(b)
 
             def pieces(n, carry):
-                to = jnp.where(n & 3 < 2, far, 3 - far)
+                to = jnp.where(n & 3 < 2, 3 - far, far)
                 send_piece(s, to + TA * ((n + 1) & 1), n >> 2, size)
                 return carry
 

time: 67.8 us -> 65.8 us (0.971)
  the two profiles are of different devices: /device:TPU:20 before, /device:TPU:1 now
where the time goes in v5:
time: 65.8 us; the launch traced here: 65.6 us
  Pallas kernels  65.6 us (100%)
    pallas_call x1, Pallas kernels, fused(): pl.pallas_call(functools.partial(fused_kernel, scale), out_shape=(jax.Sha...  60.6 us
    pallas_call x1, Pallas kernels, last_step(): pl.pallas_call(last_kernel, grid=(LAST_STEPS,), out_shape=jax.ShapeDtypeS...  5.04 us

profile of v5, /device:TPU:1, one launch (start us, length us, event | category | flops | bytes accessed | tf_op | source)
XLA Modules:
  0.0 65.6 jit_solution(18391534143351092949)
XLA Ops:
  0.0 60.6 %fused.1 = (bf16[8,256,512]{2,1,0:T(8,128)(2,1)}, bf16[32,512]{1,0:T(8,128)(2,1)}) custom-call(bf16[8,64,2048]{2,1,0:T(8,128)(2,1)} %field_in.1, bf16[2,1024,1024]{2,1,0:T(8,128)(2,1)} %constant.10.clone.xt_in, bf16[256,128]{1,0:T(8,128)(2,1)} %constant.11.clone.tt_in, bf16[3,4,512,256]{3,2,1,0:T(8,128)(2,1)} %constant.12.clone.ty_in), custom_call_target="tpu_custom_call" | custom-call | tf_op jit(solution)/shard_map/fused/pallas_call | solution.py:357
  60.6 5.0 %last_step.1 = f32[32,64,512]{2,1,0:T(8,128)} custom-call(bf16[8,256,512]{2,1,0:T(8,128)(2,1)} %get-tuple-element.7.blocks, bf16[32,512]{1,0:T(8,128)(2,1)} %get-tuple-element.8.corner, bf16[2,256,256]{2,1,0:T(8,128)(2,1)} %constant.13.clone.rows, bf16[512,512]{1,0:T(8,128)(2,1)} %constant.14.clone.order), custom_call_target="tpu_custom_call" | custom-call | tf_op jit(solution)/shard_map/last_step/pallas_call | solution.py:404

commit v6 on v5

--- a/solution.py
+++ b/solution.py
@@ -107,7 +107,7 @@
 MESH = pl.DeviceIdType.MESH
 CHUNKS = 8
 CHUNK = DEV // CHUNKS
-PIECES = 128, 64
+PIECE = 32
 
 
 def fused_kernel(
@@ -213,11 +213,11 @@
     group = jnp.where(h == 0, g, GY - 1 - g)
     part = a + TA * h
 
-    def send_piece(s, member, piece, size):
+    def send_piece(s, member, piece):
         ta, th = member & 3, member >> 2
         tg = jnp.where(th == 0, group, GY - 1 - group)
-        rows = pl.ds(pl.multiple_of(size * piece, size), size)
-        to_rows = pl.ds(pl.multiple_of(128 * s + size * piece, size), size)
+        rows = pl.ds(pl.multiple_of(PIECE * piece, PIECE), PIECE)
+        to_rows = pl.ds(pl.multiple_of(128 * s + PIECE * piece, PIECE), PIECE)
         src = blocks.at[s, member, rows]
         dst = out.at[jnp.where(th == 0, part, 7 - part), to_rows]
 
@@ -244,7 +244,6 @@
 
     for s in range(2):
         count = 160 if s == 0 else 128
-        size = PIECES[s]
         pltpu.make_async_copy(slots.at[s, 0], rec.at[s, 0], local.at[s]).wait()
         pltpu.make_async_copy(most, most, recv.at[s]).wait()
 
@@ -316,10 +315,10 @@
 
             def pieces(n, carry):
                 to = jnp.where(n & 3 < 2, 3 - far, far)
-                send_piece(s, to + TA * ((n + 1) & 1), n >> 2, size)
+                send_piece(s, to + TA * ((n + 1) & 1), n >> 2)
                 return carry
 
-            lax.fori_loop(0, 4 * (128 // size), pieces, 0)
+            lax.fori_loop(0, 4 * (128 // PIECE), pieces, 0)
             return carry
 
         lax.fori_loop(0, 2, pair_step, 0)

time: 65.8 us -> 64.1 us (0.974)
  Pallas kernels: 65.6 us -> 64 us
    pallas_call x1, Pallas kernels: 60.6 us -> 58.9 us  [fused(): pl.pallas_call(functools.partial(fused_kernel, scale), out_shape=(jax.Sha...]
where the time goes in v6:
time: 64.1 us; the launch traced here: 64 us
  Pallas kernels  64 us (100%)
    pallas_call x1, Pallas kernels, fused(): pl.pallas_call(functools.partial(fused_kernel, scale), out_shape=(jax.Sha...  58.9 us
    pallas_call x1, Pallas kernels, last_step(): pl.pallas_call(last_kernel, grid=(LAST_STEPS,), out_shape=jax.ShapeDtypeS...  5.05 us

profile of v6, /device:TPU:1, one launch (start us, length us, event | category | flops | bytes accessed | tf_op | source)
XLA Modules:
  0.0 64.0 jit_solution(14185291478675294409)
XLA Ops:
  0.0 58.9 %fused.1 = (bf16[8,256,512]{2,1,0:T(8,128)(2,1)}, bf16[32,512]{1,0:T(8,128)(2,1)}) custom-call(bf16[8,64,2048]{2,1,0:T(8,128)(2,1)} %field_in.1, bf16[2,1024,1024]{2,1,0:T(8,128)(2,1)} %constant.10.clone.xt_in, bf16[256,128]{1,0:T(8,128)(2,1)} %constant.11.clone.tt_in, bf16[3,4,512,256]{3,2,1,0:T(8,128)(2,1)} %constant.12.clone.ty_in), custom_call_target="tpu_custom_call" | custom-call | tf_op jit(solution)/shard_map/fused/pallas_call | solution.py:356
  58.9 5.0 %last_step.1 = f32[32,64,512]{2,1,0:T(8,128)} custom-call(bf16[8,256,512]{2,1,0:T(8,128)(2,1)} %get-tuple-element.7.blocks, bf16[32,512]{1,0:T(8,128)(2,1)} %get-tuple-element.8.corner, bf16[2,256,256]{2,1,0:T(8,128)(2,1)} %constant.13.clone.rows, bf16[512,512]{1,0:T(8,128)(2,1)} %constant.14.clone.order), custom_call_target="tpu_custom_call" | custom-call | tf_op jit(solution)/shard_map/last_step/pallas_call | solution.py:403

commit v7 on v6

--- a/solution.py
+++ b/solution.py
@@ -104,7 +104,7 @@
 
 
 NT = (((1,), (1,)), ((), ()))
-MESH = pl.DeviceIdType.MESH
+MESH, LOGICAL = pl.DeviceIdType.MESH, pl.DeviceIdType.LOGICAL
 CHUNKS = 8
 CHUNK = DEV // CHUNKS
 PIECE = 32
@@ -137,7 +137,7 @@
 
     for o in range(1, DEV):
         peer = (me + o) & (DEV - 1)
-        pl.semaphore_signal(barrier, inc=1, device_id=(peer >> 5, peer & 31), device_id_type=MESH)
+        pl.semaphore_signal(barrier, inc=1, device_id=peer, device_id_type=LOGICAL)
 
     for t in range(FT):
         frame(t).wait()
@@ -176,7 +176,7 @@
                 continue
             pltpu.make_async_remote_copy(
                 src_ref=src, dst_ref=dst, send_sem=send, recv_sem=recv.at[s],
-                device_id=(2 * (y >> 1) + core, 16 * (y & 1) + 4 * z + x), device_id_type=MESH,
+                device_id=GY * (2 * (y >> 1) + core) + 16 * (y & 1) + 4 * z + x, device_id_type=LOGICAL,
             ).start()
 
     for s in range(2):
@@ -379,7 +379,7 @@
 
 def last_kernel(blocks, corner, rows, order, out, turned, below):
     mirrored = lax.axis_index("gy") >= HALF
-    rows_here = rows[jnp.where(mirrored, 1, 0)]
+    rows_here = rows[0]
     first = (lax.broadcasted_iota(jnp.int32, (8 * FR, 512), 0) % 8 == 0) & mirrored
 
     @pl.when(pl.program_id(0) == 0)
@@ -407,7 +407,7 @@
         in_specs=[
             pl.BlockSpec((LAST, 256, 512), lambda m: (m, 0, 0)),
             pl.BlockSpec((FR, 512), lambda m: (0, 0)),
-            pl.BlockSpec((2, 256, 256), lambda m: (0, 0, 0)),
+            pl.BlockSpec((1, 256, 256), lambda m: (lax.axis_index("gy") // HALF, 0, 0)),
             pl.BlockSpec((512, 512), lambda m: (0, 0)),
         ],
         out_specs=pl.BlockSpec((FR, 8 * LAST, 512), lambda m: (0, m, 0)),

time: 64.1 us -> 64 us (level)
  no operation moved by 1% of the time
where the time goes in v7:
time: 64 us; the launch traced here: 63.8 us
  Pallas kernels  63.8 us (100%)
    pallas_call x1, Pallas kernels, fused(): pl.pallas_call(functools.partial(fused_kernel, scale), out_shape=(jax.Sha...  58.8 us
    pallas_call x1, Pallas kernels, last_step(): pl.pallas_call(last_kernel, grid=(LAST_STEPS,), out_shape=jax.ShapeDtypeS...  5.02 us

profile of v7, /device:TPU:1, one launch (start us, length us, event | category | flops | bytes accessed | tf_op | source)
XLA Modules:
  0.0 63.8 jit_solution(11082469635612352271)
XLA Ops:
  0.0 58.8 %fused.1 = (bf16[8,256,512]{2,1,0:T(8,128)(2,1)}, bf16[32,512]{1,0:T(8,128)(2,1)}) custom-call(bf16[8,64,2048]{2,1,0:T(8,128)(2,1)} %field_in.1, bf16[2,1024,1024]{2,1,0:T(8,128)(2,1)} %constant.10.clone.xt_in, bf16[256,128]{1,0:T(8,128)(2,1)} %constant.11.clone.tt_in, bf16[3,4,512,256]{3,2,1,0:T(8,128)(2,1)} %constant.12.clone.ty_in), custom_call_target="tpu_custom_call" | custom-call | tf_op jit(solution)/shard_map/fused/pallas_call | solution.py:356
  58.8 5.0 %last_step.1 = f32[32,64,512]{2,1,0:T(8,128)} custom-call(bf16[8,256,512]{2,1,0:T(8,128)(2,1)} %get-tuple-element.7.blocks, bf16[32,512]{1,0:T(8,128)(2,1)} %get-tuple-element.8.corner, bf16[2,256,256]{2,1,0:T(8,128)(2,1)} %constant.13.clone.rows, bf16[512,512]{1,0:T(8,128)(2,1)} %constant.14.clone.order), custom_call_target="tpu_custom_call" | custom-call | tf_op jit(solution)/shard_map/last_step/pallas_call | solution.py:403

commit v8 on v6

--- a/solution.py
+++ b/solution.py
@@ -167,7 +167,7 @@
         k = (first + c) & 7
         total, core = k >> 1, k & 1
         for i in range(CHUNK):
-            y, x = (my_y + (i >> 2)) & 3, (my_x + i) & 3
+            y, x = (my_y + (i >> 2)) & 3, (my_x + 3 * i) & 3
             z = (total + 8 - x - y) & 3
             src = slots.at[s, 16 * k + 4 * y + x]
             dst = rec.at[s, me]
@@ -314,8 +314,8 @@
                 even_step(b)
 
             def pieces(n, carry):
-                to = jnp.where(n & 3 < 2, 3 - far, far)
-                send_piece(s, to + TA * ((n + 1) & 1), n >> 2)
+                to = jnp.where(n & 1 == 0, 3 - far, far)
+                send_piece(s, to + TA * (1 - ((n >> 1) & 1)), n >> 2)
                 return carry
 
             lax.fori_loop(0, 4 * (128 // PIECE), pieces, 0)

time: 64.1 us -> 64.2 us (level)
  no operation moved by 1% of the time
where the time goes in v8:
time: 64.2 us; the launch traced here: 64 us
  Pallas kernels  64 us (100%)
    pallas_call x1, Pallas kernels, fused(): pl.pallas_call(functools.partial(fused_kernel, scale), out_shape=(jax.Sha...  59 us
    pallas_call x1, Pallas kernels, last_step(): pl.pallas_call(last_kernel, grid=(LAST_STEPS,), out_shape=jax.ShapeDtypeS...  5.04 us

profile of v8, /device:TPU:1, one launch (start us, length us, event | category | flops | bytes accessed | tf_op | source)
XLA Modules:
  0.0 64.0 jit_solution(4530764458205915657)
XLA Ops:
  0.0 59.0 %fused.1 = (bf16[8,256,512]{2,1,0:T(8,128)(2,1)}, bf16[32,512]{1,0:T(8,128)(2,1)}) custom-call(bf16[8,64,2048]{2,1,0:T(8,128)(2,1)} %field_in.1, bf16[2,1024,1024]{2,1,0:T(8,128)(2,1)} %constant.10.clone.xt_in, bf16[256,128]{1,0:T(8,128)(2,1)} %constant.11.clone.tt_in, bf16[3,4,512,256]{3,2,1,0:T(8,128)(2,1)} %constant.12.clone.ty_in), custom_call_target="tpu_custom_call" | custom-call | tf_op jit(solution)/shard_map/fused/pallas_call | solution.py:356
  59.0 5.0 %last_step.1 = f32[32,64,512]{2,1,0:T(8,128)} custom-call(bf16[8,256,512]{2,1,0:T(8,128)(2,1)} %get-tuple-element.7.blocks, bf16[32,512]{1,0:T(8,128)(2,1)} %get-tuple-element.8.corner, bf16[2,256,256]{2,1,0:T(8,128)(2,1)} %constant.13.clone.rows, bf16[512,512]{1,0:T(8,128)(2,1)} %constant.14.clone.order), custom_call_target="tpu_custom_call" | custom-call | tf_op jit(solution)/shard_map/last_step/pallas_call | solution.py:403
